TPU v7x, 32 devices: a whole 2x2x4 slice. The times are simulated.
32 devices in a mesh: dp: 8 (over y, x, core), seq: 4 (over z).
Axes of the slice: x: 2, y: 2, z: 4, core: 2. Of those that a mesh axis runs over, the one named last changes fastest.
Arguments:
- tokens: bfloat16 [24, 1024, 768], P('dp', 'seq'), may hold values from -6 to 6
- segments: int32 [24, 1024], P('dp', 'seq'), may hold values from 0 to 7, as said below
- timesteps: int32 [24], P('dp'), may hold values from 0 to 999
- w_mod: bfloat16 [768, 4608], P(('dp', 'seq')), may hold values from -0.21875 to 0.21875
- b_mod: bfloat16 [4608], P(('dp', 'seq')), may hold values from -3 to 3
- gain_attn: bfloat16 [768], P(('dp', 'seq')), may hold values from 0.25 to 1.75
- w_qkv: bfloat16 [768, 2304], P(('dp', 'seq')), may hold values from -0.21875 to 0.21875
- w_out: bfloat16 [768, 768], P(('dp', 'seq')), may hold values from -1.75 to 1.75
- gain_mlp: bfloat16 [768], P(('dp', 'seq')), may hold values from 0.25 to 1.75
- w_up: bfloat16 [768, 3072], P(('dp', 'seq')), may hold values from -0.21875 to 0.21875
- w_down: bfloat16 [3072, 768], P(('dp', 'seq')), may hold values from -0.109375 to 0.109375
- cotangent: bfloat16 [24, 1024, 768], P('dp', 'seq'), may hold values from -6 to 6
Outputs:
- output: bfloat16 [24, 1024, 768], P('dp', 'seq')
- d_tokens: bfloat16 [24, 1024, 768], P('dp', 'seq')
- g_w_mod: float32 [768, 4608], P(('dp', 'seq'))
- g_b_mod: float32 [4608], P(('dp', 'seq'))
- g_gain_attn: float32 [768], P(('dp', 'seq'))
- g_w_qkv: float32 [768, 2304], P(('dp', 'seq'))
- g_w_out: float32 [768, 768], P(('dp', 'seq'))
- g_gain_mlp: float32 [768], P(('dp', 'seq'))
- g_w_up: float32 [768, 3072], P(('dp', 'seq'))
- g_w_down: float32 [3072, 768], P(('dp', 'seq'))
Inputs may be any that keep to these rules, and one draw needn't show every extreme that they name: `segments`: in each row segment numbers start at 0 and never fall from one position to the next; a token attends only to tokens of its own segment.
All inputs are finite; a program needn't handle non-finite values.
Results may differ from a plain program's by a relative error of at most 0.018.
Values may be sent and summed in bfloat16 or wider, within the bound.
A program may use at most 192 MiB of HBM per device.

v0:
```python
import math

import jax
import jax.numpy as jnp
from jax import lax
from jax.sharding import PartitionSpec as P

HEAD_DIM = 64


EPSILON = 1e-06
MASK_FILL = -1e30


def time_embed(step_ids, model_dim):
    half_dim = model_dim // 2
    frequency = jnp.exp(-math.log(10000.0) * jnp.arange(half_dim, dtype=jnp.float32) / half_dim)
    angles = step_ids.astype(jnp.float32)[:, None] * frequency[None, :]
    return jnp.concatenate([jnp.cos(angles), jnp.sin(angles)], axis=-1)


def rotary_tables(positions, half_dim):
    frequency = jnp.exp(-math.log(10000.0) * jnp.arange(half_dim, dtype=jnp.float32) / half_dim)
    angles = positions.astype(jnp.float32)[:, None] * frequency[None, :]
    cosine = jnp.concatenate([jnp.cos(angles), jnp.cos(angles)], -1)[:, None, None, :]
    sine_table = jnp.concatenate([jnp.sin(angles), jnp.sin(angles)], -1)[:, None, None, :]
    return (cosine, sine_table)


def rotate(paired, positions):
    half_dim = paired.shape[-1] // 2
    cosine, sine_table = rotary_tables(positions, half_dim)
    front_half = paired[..., :half_dim]
    back_half = paired[..., half_dim:]
    turned = jnp.concatenate([-back_half, front_half], -1)
    return paired * cosine + turned * sine_table


def rotate_back(grads_in, positions):
    half_dim = grads_in.shape[-1] // 2
    cosine, sine_table = rotary_tables(positions, half_dim)
    scaled = grads_in * sine_table
    turned = jnp.concatenate([scaled[..., half_dim:], -scaled[..., :half_dim]], -1)
    return grads_in * cosine + turned


def modulate(inputs, norm_gain, mod_scale, mod_shift):
    average = jnp.mean(inputs, -1, keepdims=True)
    centred = inputs - average
    variance = jnp.mean(centred * centred, -1, keepdims=True)
    return centred * lax.rsqrt(variance + EPSILON) * norm_gain * (1.0 + mod_scale) + mod_shift


def scores_of(queries, keys_all, doc_ids):
    score_scale = 1.0 / math.sqrt(HEAD_DIM)
    scores = (
        jnp.einsum("qhd,khd->hqk", queries, keys_all, preferred_element_type=jnp.float32)
        * score_scale
    )
    same_doc = doc_ids[:, None] == doc_ids[None, :]
    return jnp.where(same_doc[None], scores, MASK_FILL)


def split_heads(element):
    seq_len = element.shape[0]
    split = element.reshape(seq_len, 3, -1, HEAD_DIM)
    return (split[:, 0], split[:, 1], split[:, 2])


def attend_forward(element):
    packed_row, doc_ids = element
    seq_len = packed_row.shape[0]
    queries, keys_all, values = split_heads(packed_row)
    scores = scores_of(queries, keys_all, doc_ids)
    row_max = jnp.max(scores, -1, keepdims=True)
    raised = jnp.exp(scores - row_max)
    summed = jnp.sum(raised, -1, keepdims=True)
    attn_probs = (raised / summed).astype(jnp.bfloat16)
    mixed = jnp.einsum("hqk,khd->qhd", attn_probs, values, preferred_element_type=jnp.float32)
    return (mixed.reshape(seq_len, -1).astype(jnp.bfloat16), (row_max + jnp.log(summed))[..., 0])


def attend_backward(element):
    packed_row, doc_ids, logsum, grad_row = element
    seq_len = packed_row.shape[0]
    score_scale = 1.0 / math.sqrt(HEAD_DIM)
    queries, keys_all, values = split_heads(packed_row)
    scores = scores_of(queries, keys_all, doc_ids)
    attn_probs = jnp.exp(scores - logsum[..., None])
    grad_split = grad_row.reshape(seq_len, -1, HEAD_DIM)
    grad_probs = jnp.einsum("qhd,khd->hqk", grad_split, values, preferred_element_type=jnp.float32)
    grad_values = jnp.einsum(
        "hqk,qhd->khd",
        attn_probs.astype(jnp.bfloat16),
        grad_split,
        preferred_element_type=jnp.float32,
    )
    inner_sum = jnp.sum(attn_probs * grad_probs, -1, keepdims=True)
    grad_scores = (attn_probs * (grad_probs - inner_sum)).astype(jnp.bfloat16)
    grad_queries = (
        jnp.einsum("hqk,khd->qhd", grad_scores, keys_all, preferred_element_type=jnp.float32)
        * score_scale
    )
    grad_keys = (
        jnp.einsum("hqk,qhd->khd", grad_scores, queries, preferred_element_type=jnp.float32)
        * score_scale
    )
    stacked = jnp.stack([grad_queries, grad_keys, grad_values], 1)
    return stacked.reshape(seq_len, 3, -1).astype(jnp.bfloat16)


def attention_front(stream, params, mod_parts, positions):
    local_rows, local_len, model_dim = stream.shape
    normed_a = modulate(stream, params[2].astype(jnp.float32), mod_parts[1], mod_parts[0])
    normed_a = normed_a.astype(jnp.bfloat16).reshape(local_rows * local_len, model_dim)
    qkv_proj = jnp.dot(normed_a, params[3], preferred_element_type=jnp.float32)
    qkv_proj = qkv_proj.reshape(local_rows, local_len, 3, model_dim // HEAD_DIM, HEAD_DIM)
    turned = rotate(qkv_proj[:, :, :2], positions)
    packed = jnp.concatenate([turned, qkv_proj[:, :, 2:]], 2).astype(jnp.bfloat16)
    return (normed_a, packed.reshape(local_rows, local_len, 3, model_dim))


def branch_rest(stream, mixed_rows, params, mod_parts):
    local_rows, local_len, model_dim = stream.shape
    attn_out = jnp.dot(
        mixed_rows.reshape(local_rows * local_len, model_dim),
        params[4],
        preferred_element_type=jnp.float32,
    ).reshape(local_rows, local_len, model_dim)
    middle = stream + mod_parts[2] * attn_out
    normed_m = modulate(middle, params[5].astype(jnp.float32), mod_parts[4], mod_parts[3])
    normed_m = normed_m.astype(jnp.bfloat16).reshape(local_rows * local_len, model_dim)
    up_proj = jnp.dot(normed_m, params[6], preferred_element_type=jnp.float32)
    activated = jax.nn.gelu(up_proj).astype(jnp.bfloat16)
    mlp_out = jnp.dot(activated, params[7], preferred_element_type=jnp.float32).reshape(
        local_rows, local_len, model_dim
    )
    return (attn_out, middle, normed_m, up_proj, activated, mlp_out)


def shards(
    tokens,
    segments,
    timesteps,
    w_mod,
    b_mod,
    gain_attn,
    w_qkv,
    w_out,
    gain_mlp,
    w_up,
    w_down,
    cotangent,
):
    local_rows, local_len, model_dim = tokens.shape
    head_count = model_dim // HEAD_DIM
    whole_docs = lax.all_gather(segments, "seq", axis=1, tiled=True)
    gathered = (
        lax.all_gather(w_mod, ("dp", "seq"), axis=0, tiled=True),
        lax.all_gather(b_mod, ("dp", "seq"), axis=0, tiled=True),
        lax.all_gather(gain_attn, ("dp", "seq"), axis=0, tiled=True),
        lax.all_gather(w_qkv, ("dp", "seq"), axis=0, tiled=True),
        lax.all_gather(w_out, ("dp", "seq"), axis=0, tiled=True),
        lax.all_gather(gain_mlp, ("dp", "seq"), axis=0, tiled=True),
        lax.all_gather(w_up, ("dp", "seq"), axis=0, tiled=True),
        lax.all_gather(w_down, ("dp", "seq"), axis=0, tiled=True),
    )
    embedding = time_embed(timesteps, model_dim).astype(jnp.bfloat16)
    modulation = jnp.dot(embedding, gathered[0], preferred_element_type=jnp.float32) + gathered[
        1
    ].astype(jnp.float32)
    mod_parts = [
        modulation[:, None, part * model_dim : (part + 1) * model_dim] for part in range(6)
    ]
    positions = lax.axis_index("seq") * local_len + jnp.arange(local_len, dtype=jnp.int32)
    stream = tokens.astype(jnp.float32)
    normed_a, packed = attention_front(stream, gathered, mod_parts, positions)
    spread = lax.all_to_all(packed, "seq", split_axis=3, concat_axis=1, tiled=True)
    heads_out, logsum = lax.map(attend_forward, (spread, whole_docs))
    mixed_rows = lax.all_to_all(heads_out, "seq", split_axis=1, concat_axis=2, tiled=True)
    attn_out, middle, normed_m, up_proj, activated, mlp_out = branch_rest(
        stream, mixed_rows, gathered, mod_parts
    )
    output = (middle + mod_parts[5] * mlp_out).astype(jnp.bfloat16)
    regathered = (
        lax.all_gather(w_mod, ("dp", "seq"), axis=0, tiled=True),
        lax.all_gather(b_mod, ("dp", "seq"), axis=0, tiled=True),
        lax.all_gather(gain_attn, ("dp", "seq"), axis=0, tiled=True),
        lax.all_gather(w_qkv, ("dp", "seq"), axis=0, tiled=True),
        lax.all_gather(w_out, ("dp", "seq"), axis=0, tiled=True),
        lax.all_gather(gain_mlp, ("dp", "seq"), axis=0, tiled=True),
        lax.all_gather(w_up, ("dp", "seq"), axis=0, tiled=True),
        lax.all_gather(w_down, ("dp", "seq"), axis=0, tiled=True),
    )
    normed_a, packed = attention_front(stream, regathered, mod_parts, positions)
    spread = lax.all_to_all(packed, "seq", split_axis=3, concat_axis=1, tiled=True)
    heads_out, logsum = lax.map(attend_forward, (spread, whole_docs))
    mixed_rows = lax.all_to_all(heads_out, "seq", split_axis=1, concat_axis=2, tiled=True)
    attn_out, middle, normed_m, up_proj, activated, mlp_out = branch_rest(
        stream, mixed_rows, regathered, mod_parts
    )
    grad_final = cotangent.astype(jnp.float32)
    grad_mlp = (
        (grad_final * mod_parts[5]).astype(jnp.bfloat16).reshape(local_rows * local_len, model_dim)
    )
    grad_gate_m = jnp.sum(grad_final * mlp_out, 1)
    grad_down = jnp.einsum("tf,td->fd", activated, grad_mlp, preferred_element_type=jnp.float32)
    grad_act = jnp.einsum("td,fd->tf", grad_mlp, regathered[7], preferred_element_type=jnp.float32)
    _, gelu_back = jax.vjp(jax.nn.gelu, up_proj)
    grad_up = gelu_back(grad_act)[0].astype(jnp.bfloat16)
    grad_wup = jnp.einsum("td,tf->df", normed_m, grad_up, preferred_element_type=jnp.float32)
    grad_hm = jnp.einsum("tf,df->td", grad_up, regathered[6], preferred_element_type=jnp.float32)
    grad_hm = grad_hm.reshape(local_rows, local_len, model_dim)
    _, norm_back_m = jax.vjp(
        modulate, middle, regathered[5].astype(jnp.float32), mod_parts[4], mod_parts[3]
    )
    grad_mid_norm, grad_gain_m, grad_scale_m, grad_shift_m = norm_back_m(grad_hm)
    grad_mid = grad_final + grad_mid_norm
    grad_gate_a = jnp.sum(grad_mid * attn_out, 1)
    grad_attn = (
        (grad_mid * mod_parts[2]).astype(jnp.bfloat16).reshape(local_rows * local_len, model_dim)
    )
    flat_mixed = mixed_rows.reshape(local_rows * local_len, model_dim)
    grad_wout = jnp.einsum("td,te->de", flat_mixed, grad_attn, preferred_element_type=jnp.float32)
    grad_mixed = jnp.einsum(
        "te,de->td", grad_attn, regathered[4], preferred_element_type=jnp.float32
    )
    grad_mixed = grad_mixed.astype(jnp.bfloat16).reshape(local_rows, local_len, model_dim)
    grad_heads = lax.all_to_all(grad_mixed, "seq", split_axis=2, concat_axis=1, tiled=True)
    grad_packed = lax.map(attend_backward, (spread, whole_docs, logsum, grad_heads))
    grad_rows = lax.all_to_all(grad_packed, "seq", split_axis=1, concat_axis=3, tiled=True)
    grad_rows = grad_rows.astype(jnp.float32).reshape(
        local_rows, local_len, 3, head_count, HEAD_DIM
    )
    grad_turned = rotate_back(grad_rows[:, :, :2], positions)
    grad_qkv = jnp.concatenate([grad_turned, grad_rows[:, :, 2:]], 2)
    grad_qkv = grad_qkv.reshape(local_rows * local_len, 3 * model_dim).astype(jnp.bfloat16)
    grad_wqkv = jnp.einsum("td,te->de", normed_a, grad_qkv, preferred_element_type=jnp.float32)
    grad_ha = jnp.einsum("te,de->td", grad_qkv, regathered[3], preferred_element_type=jnp.float32)
    grad_ha = grad_ha.reshape(local_rows, local_len, model_dim)
    _, norm_back_a = jax.vjp(
        modulate, stream, regathered[2].astype(jnp.float32), mod_parts[1], mod_parts[0]
    )
    grad_in_norm, grad_gain_a, grad_scale_a, grad_shift_a = norm_back_a(grad_ha)
    grad_input = (grad_mid + grad_in_norm).astype(jnp.bfloat16)
    grad_mod = jnp.concatenate(
        [
            grad_shift_a.reshape(local_rows, model_dim),
            grad_scale_a.reshape(local_rows, model_dim),
            grad_gate_a,
            grad_shift_m.reshape(local_rows, model_dim),
            grad_scale_m.reshape(local_rows, model_dim),
            grad_gate_m,
        ],
        -1,
    )
    grad_wmod = jnp.dot(
        embedding.astype(jnp.float32).T,
        grad_mod,
        precision=lax.Precision.HIGHEST,
        preferred_element_type=jnp.float32,
    )
    grad_bmod = jnp.sum(grad_mod, 0)
    summed = (
        lax.psum_scatter(grad_wmod, ("dp", "seq"), scatter_dimension=0, tiled=True),
        lax.psum_scatter(grad_bmod, ("dp", "seq"), scatter_dimension=0, tiled=True),
        lax.psum_scatter(grad_gain_a, ("dp", "seq"), scatter_dimension=0, tiled=True),
        lax.psum_scatter(grad_wqkv, ("dp", "seq"), scatter_dimension=0, tiled=True),
        lax.psum_scatter(grad_wout, ("dp", "seq"), scatter_dimension=0, tiled=True),
        lax.psum_scatter(grad_gain_m, ("dp", "seq"), scatter_dimension=0, tiled=True),
        lax.psum_scatter(grad_wup, ("dp", "seq"), scatter_dimension=0, tiled=True),
        lax.psum_scatter(grad_down, ("dp", "seq"), scatter_dimension=0, tiled=True),
    )
    return (
        output,
        grad_input,
        summed[0],
        summed[1],
        summed[2],
        summed[3],
        summed[4],
        summed[5],
        summed[6],
        summed[7],
    )


def solution(mesh):
    placed = (
        P("dp", "seq", None),
        P("dp", "seq"),
        P("dp"),
        P(("dp", "seq"), None),
        P(("dp", "seq")),
        P(("dp", "seq")),
        P(("dp", "seq"), None),
        P(("dp", "seq"), None),
        P(("dp", "seq")),
        P(("dp", "seq"), None),
        P(("dp", "seq"), None),
        P("dp", "seq", None),
    )
    return jax.shard_map(
        shards,
        mesh=mesh,
        in_specs=placed,
        out_specs=(
            P("dp", "seq", None),
            P("dp", "seq", None),
            P(("dp", "seq"), None),
            P(("dp", "seq")),
            P(("dp", "seq")),
            P(("dp", "seq"), None),
            P(("dp", "seq"), None),
            P(("dp", "seq")),
            P(("dp", "seq"), None),
            P(("dp", "seq"), None),
        ),
        check_vma=False,
    )
```

profile of v0, /device:TPU:24, one launch (start us, length us, event | category | flops | bytes accessed | tf_op | source)
XLA Modules:
  0.0 1273.8 jit_solution(16889937688959112797)
XLA Ops:
  14.7 39.5 %all-reduce.7 = (bf16[4608]{0:T(1024)(128)(2,1)S(1)}, bf16[768]{0:T(1024)(128)(2,1)S(1)}, bf16[768]{0:T(1024)(128)(2,1)}) all-reduce(bf16[4608]{0:T(1024)(128)(2,1)S(1)} %dynamic-update-slice, bf16[768]{0:T(1024)(128)(2,1)S(1)} %dynamic-update-slice.1, bf16[768]{0:T(1024)(128)(2,1)S(1)} %dynamic-update-slice.2), channel_id=1, replica_groups=mesh['dp'=8,'seq'=4] {'dp','seq'}, use_global_device_ids=true, to_apply=%add | all-reduce | flops 6144 | bytes 24576
  55.8 15.0 %all-gather.8.cloned.1.call-done = bf16[768,2304]{1,0:T(8,128)(2,1)} async-done(((bf16[24,2304]{1,0:T(8,128)(2,1)}), bf16[768,2304]{1,0:T(8,128)(2,1)}) %all-gather.8.cloned.1.call-update) | async-done | bytes 3538960 | tf_op jit(solution)/shard_map/all_gather | solution.py:162
  70.8 5.9 copy.98
  76.7 68.1 %all-gather.6.cloned.1.call-done = bf16[768,4608]{1,0:T(8,128)(2,1)} async-done(((bf16[24,4608]{1,0:T(8,128)(2,1)}), bf16[768,4608]{1,0:T(8,128)(2,1)}) %all-gather.6.cloned.1.call-update) | async-done | bytes 7077904 | tf_op jit(solution)/shard_map/all_gather | solution.py:159
  144.8 4.2 convolution_add_fusion
  160.2 7.3 pad_maximum_fusion
  167.4 7.0 all-to-all-start
  175.0 115.5 %all_gather.37 = s32[3,1024]{1,0:T(4,128)S(1)} all-gather(s32[3,256]{1,0:T(4,128)S(1)} %copy-done.64), channel_id=1, replica_groups=mesh['dp'=8,'seq'=4] {'seq'}, dimensions={1}, use_global_device_ids=true | all-gather | bytes 15360 | tf_op jit(solution)/shard_map/all_gather | solution.py:157
  290.6 5.8 copy.101
  296.4 4.6 all_to_all.63
  302.1 46.1 %while.33 = (s32[]{:T(128)}, bf16[3,1024,192]{1,2,0:T(8,128)(2,1)}, f32[3,3,1024]{2,1,0:T(4,128)}, bf16[3,1024,3,192]{1,3,2,0:T(8,128)(2,1)}, s32[3,1024]{1,0:T(4,128)S(1)}, /*index=5*/s32[]{:T(128)}) while((s32[]{:T(128)}, bf16[3,1024,192]{1,2,0:T(8,128)(2,1)}, f32[3,3,1024]{2,1,0:T(4,128)}, bf16[3,1024,3,192]{1,3,2,0:T(8,128)(2,1)}, ...), condition=%wide.region_11.12_spmd, body=%wide.region_8.11_spmd.sunk | while | flops 844297216 | bytes 55689364 | solution.py:197
  307.2 3.9 fusion.147
  311.0 5.0 fusion.148
  322.5 3.9 fusion.147
  326.4 5.1 fusion.148
  338.0 3.9 fusion.147
  341.8 5.0 fusion.148
  348.3 4.1 copy.106
  352.3 5.7 all-to-all-start.2
  358.1 47.2 %while.32 = (s32[]{:T(128)}, bf16[3,1024,192]{1,2,0:T(8,128)(2,1)S(1)}, bf16[3,1024,3,192]{1,3,2,0:T(8,128)(2,1)}, s32[3,1024]{1,0:T(4,128)S(1)}, s32[]{:T(128)}) while((s32[]{:T(128)}, bf16[3,1024,192]{1,2,0:T(8,128)(2,1)S(1)}, bf16[3,1024,3,192]{1,3,2,0:T(8,128)(2,1)}, s32[3,1024]{1,0:T(4,128)S(1)}, s32[]{:T(128)}) %tuple.113), condition=%wide.region_5.6_spmd, body=%wide.region_2.5_spmd.sunk | while | flops 825426944 | bytes 32022608 | solution.py:179
  360.2 7.6 fusion.144
  367.8 5.8 fusion.145
  375.7 7.6 fusion.144
  383.3 6.4 fusion.145
  391.8 7.6 fusion.144
  399.4 5.8 fusion.145
  407.8 13.4 %all-to-all-done.2 = bf16[3,1024,192]{2,0,1:T(4,128)(2,1)} async-done(((bf16[3,1024,192]{2,0,1:T(4,128)(2,1)}), bf16[3,1024,192]{2,0,1:T(4,128)(2,1)}, u32[]{:S(2)}, u32[]{:S(2)}) %all-to-all-start.2) | async-done | bytes 1179680 | tf_op jit(solution)/shard_map/all_to_all | solution.py:198
  421.2 5.9 all-to-all-start.1
  427.8 4.2 copy.108
  431.9 4.3 copy.117
  436.3 36.6 %all-to-all-done.1 = bf16[3,1024,192]{2,0,1:T(4,128)(2,1)S(1)} async-done(((bf16[3,1024,192]{2,0,1:T(4,128)(2,1)}), bf16[3,1024,192]{2,0,1:T(4,128)(2,1)S(1)}, u32[]{:S(2)}, u32[]{:S(2)}) %all-to-all-start.1) | async-done | bytes 1179680 | tf_op jit(solution)/shard_map/all_to_all | solution.py:180
  475.1 4.1 reshape.410
  487.6 3.4 add_convert_fusion.1
  491.1 13.4 %fusion.49 = f32[768,768]{1,0:T(8,128)} fusion(bf16[3072,768]{1,0:T(8,128)(2,1)} %all-gather.14.cloned.1.call-done, bf16[768,768]{1,0:T(8,128)(2,1)} %bitcast.275, bf16[768,3072]{1,0:T(8,128)(2,1)} %all-gather.12.cloned.1.call-done), kind=kOutput, calls=%fused_computation.90 | convolution fusion | flops 7268990976 | bytes 12976128 | tf_op jit(solution)/shard_map/dot_general | solution.py:135
  504.5 4.0 fusion.65
  508.5 3.8 fusion.96
  512.4 11.0 fusion.38
  523.4 3.8 fusion.97
  536.2 8.6 fusion.100
  548.2 3.7 copy.110
  551.9 5.9 all-to-all-start.3
  557.8 12.7 fusion.86
  570.8 27.4 %all-to-all-done.3 = bf16[3,256,768]{1,0,2:T(4,128)(2,1)S(1)} async-done(((bf16[3,256,768]{1,0,2:T(4,128)(2,1)}), bf16[3,256,768]{1,0,2:T(4,128)(2,1)S(1)}, u32[]{:S(2)}, u32[]{:S(2)}) %all-to-all-start.3) | async-done | bytes 1179680 | tf_op jit(solution)/shard_map/all_to_all | solution.py:229
  598.5 80.8 %while.34 = (s32[]{:T(128)}, bf16[3,1024,3,192]{1,3,2,0:T(8,128)(2,1)}, bf16[3,1024,3,192]{1,3,2,0:T(8,128)(2,1)}, s32[3,1024]{1,0:T(4,128)S(1)}, f32[3,3,1024]{...) while((s32[]{:T(128)}, bf16[3,1024,3,192]{1,3,2,0:T(8,128)(2,1)}, ...), condition=%wide.region_18.19_spmd, body=%wide.region_16.18_spmd.sunk | while | flops 2066019328 | bytes 108105824 | solution.py:230
  603.2 3.7 fusion.155
  606.9 7.1 multiply_reduce_fusion.8
  614.0 7.0 multiply_convert_fusion.6
  630.0 3.7 fusion.155
  633.7 7.1 multiply_reduce_fusion.8
  640.8 6.9 multiply_convert_fusion.6
  656.8 3.7 fusion.155
  660.6 7.1 multiply_reduce_fusion.8
  667.6 7.4 multiply_convert_fusion.6
  679.4 10.0 copy.113
  689.4 184.6 %all_to_all.80 = bf16[3,1024,3,192]{3,2,0,1:T(4,128)(2,1)} all-to-all(bf16[3,1024,3,192]{3,2,0,1:T(4,128)(2,1)} %copy.113), channel_id=1, replica_groups=mesh['dp'=8,'seq'=4] {'seq'}, dimensions={1} | all-to-all | bytes 7077888 | tf_op jit(solution)/shard_map/all_to_all | solution.py:231
  874.0 11.1 copy.114
  892.6 3.4 copy.116
  897.3 5.0 fusion.98
  902.7 9.8 fusion.87
  912.5 3.4 fusion.68
  920.8 8.9 fusion.79
  930.3 41.0 %all-reduce.6 = (f32[4608]{0:T(1024)S(1)}, f32[768]{0:T(1024)S(1)}, f32[768]{0:T(1024)S(1)}) all-reduce(f32[4608]{0:T(1024)S(1)} %reduce_sum.222, f32[768]{0:T(1024)S(1)} %get-tuple-element.99, f32[768]{0:T(1024)S(1)} %copy-done.63), channel_id=3, replica_groups=mesh['dp'=8,'seq'=4] {'dp','seq'}, use_global_device_ids=true, to_apply=%region_29.30.clone | all-reduce | flops 6144 | bytes 49152
  973.3 125.4 %reduce-scatter.8.cloned.1.call-done = f32[24,2304]{1,0:T(8,128)} async-done(((f32[768,2304]{1,0:T(8,128)}), f32[24,2304]{1,0:T(8,128)}) %reduce-scatter.8.cloned.1.call-update) | async-done | bytes 221200 | tf_op jit(solution)/shard_map/reduce_scatter | solution.py:268
  1098.7 167.9 %reduce-scatter.6.cloned.1.call-done = f32[24,4608]{1,0:T(8,128)} async-done(((f32[768,4608]{1,0:T(8,128)}), f32[24,4608]{1,0:T(8,128)}) %reduce-scatter.6.cloned.1.call-update) | async-done | bytes 442384 | tf_op jit(solution)/shard_map/reduce_scatter | solution.py:265
  (307 shorter events, 116.9 us)
Async XLA Ops:
  7.2 47.4 %copy-start.1 = (bf16[3,256,768]{2,1,0:T(8,128)(2,1)S(1)}, bf16[3,256,768]{2,1,0:T(8,128)(2,1)}, u32[]{:S(2)}) copy-start(bf16[3,256,768]{2,1,0:T(8,128)(2,1)} %param.18) | copy-start | bytes 3538948
  7.2 63.6 %all-gather.8.cloned.1.call-start = ((), (), s32[]{:S(2)}) async-start(), calls=%async_computation.11 | async-start | bytes 3649536 | tf_op jit(solution)/shard_map/all_gather | solution.py:162
  7.9 136.9 %all-gather.6.cloned.1.call-start = ((), (), s32[]{:S(2)}) async-start(), calls=%async_computation.10 | async-start | bytes 7299072 | tf_op jit(solution)/shard_map/all_gather | solution.py:159
  8.7 470.6 %all-gather.10.cloned.1.call-start = ((), (), s32[]{:S(2)}) async-start(), calls=%async_computation.12 | async-start | bytes 1216512 | tf_op jit(solution)/shard_map/all_gather | solution.py:163
  9.4 481.6 %all-gather.12.cloned.1.call-start = ((), (), s32[]{:S(2)}) async-start(), calls=%async_computation.13 | async-start | bytes 4866048 | tf_op jit(solution)/shard_map/all_gather | solution.py:165
  54.3 95.3 %copy-start.46 = (f32[768]{0:T(1024)}, f32[768]{0:T(1024)S(1)}, u32[]{:S(2)}) copy-start(f32[768]{0:T(1024)S(1)} %convert_element_type.154) | copy-start | bytes 9220
  54.5 101.9 %copy-start.27 = (f32[256,64]{0,1:T(8,128)}, f32[256,64]{0,1:T(8,128)S(1)}, u32[]{:S(2)}) copy-start(f32[256,64]{0,1:T(8,128)S(1)} %get-tuple-element.178) | copy-start | bytes 196612
  54.5 101.9 %copy-start.29 = (f32[256,64]{0,1:T(8,128)}, f32[256,64]{0,1:T(8,128)S(1)}, u32[]{:S(2)}) copy-start(f32[256,64]{0,1:T(8,128)S(1)} %get-tuple-element.179) | copy-start | bytes 196612
  54.5 95.1 %copy-start.40 = (f32[3,256]{1,0:T(4,128)}, f32[3,256]{1,0:T(4,128)S(1)}, u32[]{:S(2)}) copy-start(f32[3,256]{1,0:T(4,128)S(1)} %broadcast_multiply_fusion.2) | copy-start | bytes 9220
  55.6 94.0 %copy-start.48 = (f32[3,256]{1,0:T(4,128)}, f32[3,256]{1,0:T(4,128)S(1)}, u32[]{:S(2)}) copy-start(f32[3,256]{1,0:T(4,128)S(1)} %fusion.77) | copy-start | bytes 9220
  55.8 89.0 %copy-start.59 = (bf16[3,384]{1,0:T(4,128)(2,1)}, bf16[3,384]{1,0:T(4,128)(2,1)S(1)}, u32[]{:S(2)}) copy-start(bf16[3,384]{1,0:T(4,128)(2,1)S(1)} %get-tuple-element.167) | copy-start | bytes 6916
  55.8 89.0 %copy-start.61 = (bf16[3,384]{1,0:T(4,128)(2,1)}, bf16[3,384]{1,0:T(4,128)(2,1)S(1)}, u32[]{:S(2)}) copy-start(bf16[3,384]{1,0:T(4,128)(2,1)S(1)} %get-tuple-element.168) | copy-start | bytes 6916
  144.8 5.7 copy-start.18
  149.6 3.9 copy-start.33
  150.5 3.0 copy-start.22
  167.4 7.6 copy-start.64
  167.4 123.1 %all-to-all-start = ((bf16[3,256,3,768]{1,2,0,3:T(4,128)(2,1)}), bf16[3,256,3,768]{1,2,0,3:T(4,128)(2,1)}, u32[]{:S(2)}, u32[]{:S(2)}) async-start(bf16[3,256,3,768]{1,2,0,3:T(4,128)(2,1)} %pad_maximum_fusion), calls=%async_computation | async-start | bytes 9437184 | tf_op jit(solution)/shard_map/all_to_all | solution.py:178
  174.5 316.6 %all-gather.14.cloned.1.call-start = ((), (), s32[]{:S(2)}) async-start(), calls=%async_computation.14 | async-start | bytes 4866048 | tf_op jit(solution)/shard_map/all_gather | solution.py:166
  302.8 4.4 copy-start
  318.1 4.4 copy-start
  333.6 4.4 copy-start
  352.3 68.9 %all-to-all-start.2 = ((bf16[3,1024,192]{2,0,1:T(4,128)(2,1)}), bf16[3,1024,192]{2,0,1:T(4,128)(2,1)}, u32[]{:S(2)}, u32[]{:S(2)}) async-start(bf16[3,1024,192]{2,0,1:T(4,128)(2,1)} %copy.106), calls=%async_computation.2 | async-start | bytes 4194304 | tf_op jit(solution)/shard_map/all_to_all | solution.py:198
  407.8 19.3 %copy-start.65 = (bf16[768]{0:T(1024)(128)(2,1)S(1)}, bf16[768]{0:T(1024)(128)(2,1)}, u32[]{:S(2)}) copy-start(bf16[768]{0:T(1024)(128)(2,1)} %get-tuple-element.141) | copy-start | bytes 4612
  421.2 51.6 %all-to-all-start.1 = ((bf16[3,1024,192]{2,0,1:T(4,128)(2,1)}), bf16[3,1024,192]{2,0,1:T(4,128)(2,1)S(1)}, u32[]{:S(2)}, u32[]{:S(2)}) async-start(bf16[3,1024,192]{2,0,1:T(4,128)(2,1)} %copy.102), calls=%async_computation.1 | async-start | bytes 4194304 | tf_op jit(solution)/shard_map/all_to_all | solution.py:180
  427.2 545.9 %reduce-scatter.10.cloned.1.call-start = ((), (), s32[]{:S(2)}) async-start(), calls=%async_computation.17 | async-start | bytes 2433024 | tf_op jit(solution)/shard_map/reduce_scatter | solution.py:269
  472.8 6.4 copy-start.2
  472.8 6.4 copy-start.35
  475.1 4.1 copy-start.21
  481.8 5.5 copy-start.7
  486.9 4.1 copy-start.38
  487.3 3.7 copy-start.57
  487.3 3.7 copy-start.44
  491.1 13.4 %copy-start.10 = (bf16[3,256,768]{2,1,0:T(8,128)(2,1)S(1)}, bf16[3,256,768]{2,1,0:T(8,128)(2,1)}, u32[]{:S(2)}) copy-start(bf16[3,256,768]{2,1,0:T(8,128)(2,1)} %param.29) | copy-start | bytes 3538948
  504.5 4.0 copy-start.66
  504.5 7.9 slice-start.2
  508.5 3.9 copy-start.19
  508.5 3.9 copy-start.15
  508.5 3.9 slice-start.3
  523.4 3.9 copy-start.14
  523.4 3.9 copy-start.32
  523.4 3.9 copy-start.39
  523.4 3.9 copy-start.43
  523.4 3.9 copy-start.45
  534.9 438.2 %reduce-scatter.12.cloned.1.call-start = ((), (), s32[]{:S(2)}) async-start(), calls=%async_computation.18 | async-start | bytes 9732096 | tf_op jit(solution)/shard_map/reduce_scatter | solution.py:271
  548.2 9.6 copy-start.20
  551.9 46.3 %all-to-all-start.3 = ((bf16[3,256,768]{1,0,2:T(4,128)(2,1)}), bf16[3,256,768]{1,0,2:T(4,128)(2,1)S(1)}, u32[]{:S(2)}, u32[]{:S(2)}) async-start(bf16[3,256,768]{1,0,2:T(4,128)(2,1)} %copy.110), calls=%async_computation.3 | async-start | bytes 3145728 | tf_op jit(solution)/shard_map/all_to_all | solution.py:229
  557.8 415.5 %reduce-scatter.14.cloned.1.call-start = ((), (), s32[]{:S(2)}) async-start(), calls=%async_computation.19 | async-start | bytes 9732096 | tf_op jit(solution)/shard_map/reduce_scatter | solution.py:272
  570.6 528.2 %reduce-scatter.8.cloned.1.call-start = ((), (), s32[]{:S(2)}) async-start(), calls=%async_computation.16 | async-start | bytes 7299072 | tf_op jit(solution)/shard_map/reduce_scatter | solution.py:268
  885.0 5.4 slice-start
  887.0 3.5 slice-start.1
  892.6 3.4 copy-start.8
  902.3 10.2 copy-start.3
  902.3 10.2 copy-start.34
  902.3 10.2 copy-start.41
  902.3 10.2 copy-start.47
  902.3 364.3 %reduce-scatter.6.cloned.1.call-start = ((), (), s32[]{:S(2)}) async-start(), calls=%async_computation.15 | async-start | bytes 14598144 | tf_op jit(solution)/shard_map/reduce_scatter | solution.py:265
  902.6 9.9 copy-start.9
  902.7 9.9 copy-start.17
  912.5 3.5 copy-start.56
  912.5 3.5 copy-start.49
  912.5 5.4 copy-start.12
  918.0 2.7 copy-start.50
  918.0 2.8 copy-start.60
  918.0 2.8 copy-start.62
  (25 other events, 41.7 us)
Sparse Core Ops, SparseCore 0:
  10.8 59.8 all-gather.7
  73.6 71.1 all-gather.5
  147.6 111.7 all-gather.9
  262.1 66.2 all-gather.11
  331.0 86.8 all-gather.13
  535.0 99.3 reduce-scatter.9
  642.0 188.2 reduce-scatter.11
  836.7 136.5 reduce-scatter.13
  980.5 118.1 reduce-scatter.7
  1105.1 161.4 reduce-scatter.5
where the time goes:
time: 1280 us; the launch traced here: 1270 us
  waiting for transfers between devices  457 us (36%)
  blocking collectives  381 us (30%)
  matrix products  209 us (16%)
  local copies, waits for them, and re-layouts  106 us (8%)
  other arithmetic  79.5 us (6%)
  starting transfers between devices  25.2 us (2%)
  between operations  15.5 us (1%)
    all_to_all x1, blocking collectives, shards(): lax.all_to_all(grad_packed, 'seq', split_axis=1, concat_axis=3, tiled=True)  185 us
    reduce_scatter x1, waiting for transfers between devices, shards(): lax.psum_scatter(grad_wmod, ('dp', 'seq'), scatter_dimension=0, tiled=True)  168 us
    reduce_scatter x1, waiting for transfers between devices, shards(): lax.psum_scatter(grad_wqkv, ('dp', 'seq'), scatter_dimension=0, tiled=True)  125 us
    all_gather x1, blocking collectives, shards(): whole_docs = lax.all_gather(segments, 'seq', axis=1, tiled=True)  116 us
    unnamed x2, blocking collectives  80.5 us
    all_gather x1, waiting for transfers between devices, shards(): lax.all_gather(w_mod, ('dp', 'seq'), axis=0, tiled=True)  68.1 us
    all_to_all x2, waiting for transfers between devices, shards(): lax.all_to_all(heads_out, 'seq', split_axis=1, concat_axis=2, tiled=True)  49.9 us
    dot_general x6, matrix products, attend_forward(): jnp.einsum('hqk,khd->qhd', attn_probs, values, preferred_element_type=jnp...  33.2 us
  transfers between devices with their start and end apart: 14, of which 8 were waited for; matrix products, arithmetic and copies ran while one was open for 27% of the time, Pallas kernels for 0%

commit v1 on v0

v1 whole, which is shorter than its diff:
```python
import functools
import math

import jax
import jax.numpy as jnp
import numpy as np
from jax import lax
from jax.experimental import pallas as pl
from jax.experimental.pallas import tpu as pltpu
from jax.sharding import PartitionSpec as P

HEAD_DIM = 64
EPSILON = 1e-06
MASK_FILL = -1e30
MESH = pl.DeviceIdType.MESH
BF16 = jnp.bfloat16
F32 = jnp.float32
ANY = pl.BlockSpec(memory_space=pl.ANY)
VMEM = pl.BlockSpec(memory_space=pltpu.VMEM)
VMEM_LIMIT = 56 * 2**20


def place():
    return lax.axis_index("dp"), lax.axis_index("seq")


def xor(index, bits):
    return jnp.bitwise_xor(index, bits)


def remote(src, dst, send, recv, dp, seq):
    return pltpu.make_async_remote_copy(
        src_ref=src,
        dst_ref=dst,
        send_sem=send,
        recv_sem=recv,
        device_id=(dp, seq),
        device_id_type=MESH,
    )


def greet(n_dp, n_seq):
    d, s = place()
    barrier = pltpu.get_barrier_semaphore()
    for off in range(1, n_dp):
        pl.semaphore_signal(
            barrier, inc=1, device_id=(xor(d, off), s), device_id_type=MESH
        )
    for off in range(1, n_seq):
        pl.semaphore_signal(
            barrier, inc=1, device_id=(d, lax.rem(s + off, n_seq)), device_id_type=MESH
        )
    pl.semaphore_wait(barrier, n_dp - 1 + n_seq - 1)


def bit_orders(n_dp):
    high = [1 << b for b in range(1, n_dp.bit_length() - 1)]
    return (high + [1], high[::-1] + [1])


class WeightGather:
    def __init__(self, shard, full, own_sem, z_send, z_recv, x_send, x_recv, n_dp, n_seq):
        self.__dict__.update(locals())
        self.half = n_seq // 2
        self.orders = bit_orders(n_dp)
        self.groups = []
        for h in range(2):
            known = [(0, 0)]
            for step, bit in enumerate(self.orders[h]):
                known += [(off ^ bit, step + 1) for off, _ in known]
            self.groups.append(known)
        self.stages = len(self.orders[0]) + 1

    def own(self):
        d, s = place()
        return pltpu.make_async_copy(self.shard, self.full.at[d, s], self.own_sem)

    def z_copy(self, off):
        d, s = place()
        return remote(
            self.shard,
            self.full.at[d, s],
            self.z_send.at[off],
            self.z_recv.at[off],
            d,
            lax.rem(s + off, self.n_seq),
        )

    def z_wait(self, off):
        d, s = place()
        origin = lax.rem(s + self.n_seq - off, self.n_seq)
        remote(
            self.shard,
            self.full.at[d, origin],
            self.z_send.at[off],
            self.z_recv.at[off],
            d,
            origin,
        ).wait_recv()

    def x_copy(self, h, off, bit):
        d, s = place()
        part = self.full.at[xor(d, off), pl.ds(h * self.half, self.half)]
        return remote(
            part,
            part,
            self.x_send.at[h, off ^ bit],
            self.x_recv.at[h, off ^ bit],
            xor(d, bit),
            s,
        )

    def x_wait(self, h, off):
        d, s = place()
        part = self.full.at[xor(d, off), pl.ds(h * self.half, self.half)]
        remote(
            part, part, self.x_send.at[h, off], self.x_recv.at[h, off], d, s
        ).wait_recv()

    def start(self):
        self.own().start()
        for off in range(1, self.n_seq):
            self.z_copy(off).start()

    def stage(self, t):
        if t == 0:
            self.own().wait()
            for off in range(1, self.n_seq):
                self.z_wait(off)
        for h in range(2):
            for off, step in self.groups[h]:
                if step != t:
                    continue
                if t:
                    self.x_wait(h, off)
                for bit in self.orders[h][t:]:
                    self.x_copy(h, off, bit).start()

    def finish(self):
        for off in range(1, self.n_seq):
            self.z_copy(off).wait_send()
        for h in range(2):
            for off, step in self.groups[h]:
                for bit in self.orders[h][step:]:
                    self.x_copy(h, off, bit).wait_send()


def gather_kernel(n_dp, n_seq, rows, *refs):
    (tokens, cot, seg, part, *shards) = refs[:8]
    (tok_o, cot_o, seg_o, mod_o, *fulls) = refs[8:16]
    (
        zeros,
        zeros_seg,
        mod_in,
        mod_sum,
        mod_row,
        row_send,
        row_recv,
        mod_send,
        mod_recv,
        modz_send,
        modz_recv,
        own_sem,
        z_send,
        z_recv,
        x_send,
        x_recv,
    ) = refs[16:]
    d, s = place()
    first = lax.rem(d, 2)
    mine = s - first
    active = jnp.logical_and(mine >= 0, mine < rows)
    greet(n_dp, n_seq)

    def mod_copy(off):
        return remote(
            part.at[xor(d, off)],
            mod_in.at[d],
            mod_send.at[off],
            mod_recv.at[off],
            xor(d, off),
            s,
        )

    own_part = pltpu.make_async_copy(part.at[d], mod_in.at[d], mod_send.at[0])
    own_part.start()
    for off in range(1, n_dp):
        mod_copy(off).start()

    weights = [
        WeightGather(
            shards[w],
            fulls[w],
            own_sem.at[w],
            z_send.at[w],
            z_recv.at[w],
            x_send.at[w],
            x_recv.at[w],
            n_dp,
            n_seq,
        )
        for w in range(4)
    ]
    weights[0].start()

    trio = ((tokens, tok_o), (seg, seg_o), (cot, cot_o))

    def row_start(k):
        src, dst = trio[k]
        for i in range(rows):
            owner = first + i
            args = (src.at[i], dst.at[s], row_send.at[k, i])

            @pl.when(owner == s)
            def _():
                pltpu.make_async_copy(*args).start()

            @pl.when(owner != s)
            def _():
                remote(*args, row_recv.at[k, s], d, owner).start()

    def row_finish(k):
        src, dst = trio[k]
        for i in range(rows):
            owner = first + i
            args = (src.at[i], dst.at[s], row_send.at[k, i])

            @pl.when(owner == s)
            def _():
                pltpu.make_async_copy(*args).wait()

            @pl.when(owner != s)
            def _():
                remote(*args, row_recv.at[k, s], d, owner).wait_send()

        @pl.when(active)
        def _():
            for off in range(1, n_seq):
                origin = lax.rem(s + off, n_seq)
                remote(
                    src.at[0],
                    dst.at[origin],
                    row_send.at[k, 0],
                    row_recv.at[k, origin],
                    d,
                    origin,
                ).wait_recv()

        @pl.when(jnp.logical_not(active))
        def _():
            fill = zeros_seg if k == 1 else zeros
            copies = [
                pltpu.make_async_copy(fill, dst.at[z], row_recv.at[k, z])
                for z in range(n_seq)
            ]
            for c in copies:
                c.start()
            for c in copies:
                c.wait()

    zeros[...] = jnp.zeros_like(zeros)
    zeros_seg[...] = jnp.zeros_like(zeros_seg)
    row_start(0)
    row_start(1)
    for w in range(1, 4):
        weights[w].start()

    own_part.wait()
    for off in range(1, n_dp):
        remote(
            part.at[d],
            mod_in.at[xor(d, off)],
            mod_send.at[off],
            mod_recv.at[off],
            d,
            s,
        ).wait_recv()
    total = mod_in[0]
    for e in range(1, n_dp):
        total += mod_in[e]
    mod_sum[...] = total
    for i in range(rows):
        owner = first + i

        @pl.when(owner == s)
        def _():
            mod_row[s] = mod_sum[i]

        @pl.when(owner != s)
        def _():
            remote(
                mod_sum.at[i], mod_row.at[s], modz_send.at[i], modz_recv.at[s], d, owner
            ).start()

    row_start(2)
    stages = weights[0].stages
    for slot in range(stages + 3):
        for w in range(4):
            if 0 <= slot - w < stages:
                weights[w].stage(slot - w)

    @pl.when(active)
    def _():
        for off in range(1, n_seq):
            origin = lax.rem(s + off, n_seq)
            remote(
                mod_sum.at[0],
                mod_row.at[origin],
                modz_send.at[0],
                modz_recv.at[origin],
                d,
                origin,
            ).wait_recv()
        total = mod_row[0]
        for z in range(1, n_seq):
            total += mod_row[z]
        mod_o[...] = total

    @pl.when(jnp.logical_not(active))
    def _():
        mod_o[...] = jnp.zeros_like(mod_o)

    for i in range(rows):
        owner = first + i

        @pl.when(owner != s)
        def _():
            remote(
                mod_sum.at[i], mod_row.at[s], modz_send.at[i], modz_recv.at[s], d, owner
            ).wait_send()

    for off in range(1, n_dp):
        mod_copy(off).wait_send()
    for k in range(3):
        row_finish(k)
    for w in weights:
        w.finish()


def gather(n_dp, n_seq, tokens, cot, seg, part, shards):
    rows, length, width = tokens.shape
    dma = pltpu.SemaphoreType.DMA
    struct = jax.ShapeDtypeStruct
    outs = [
        struct((n_seq, length, width), BF16),
        struct((n_seq, length, width), BF16),
        struct((n_seq,) + seg.shape[1:], jnp.int32),
        struct((8, width), F32),
    ] + [struct((n_dp, n_seq) + w.shape, BF16) for w in shards]
    return pl.pallas_call(
        functools.partial(gather_kernel, n_dp, n_seq, rows),
        out_shape=outs,
        in_specs=[ANY] * 8,
        out_specs=[ANY, ANY, ANY, VMEM] + [ANY] * 4,
        scratch_shapes=[
            pltpu.VMEM((length, width), BF16),
            pltpu.VMEM(seg.shape[1:], jnp.int32),
            pltpu.VMEM((n_dp, rows, 8, width), F32),
            pltpu.VMEM((rows, 8, width), F32),
            pltpu.VMEM((n_seq, 8, width), F32),
            dma((3, rows)),
            dma((3, n_seq)),
            dma((n_dp,)),
            dma((n_dp,)),
            dma((rows,)),
            dma((n_seq,)),
            dma((4,)),
            dma((4, n_seq)),
            dma((4, n_seq)),
            dma((4, 2, n_dp)),
            dma((4, 2, n_dp)),
        ],
        compiler_params=pltpu.CompilerParams(
            collective_id=0, has_side_effects=True, vmem_limit_bytes=VMEM_LIMIT
        ),
    )(tokens, cot, seg, part, *shards)


class GradScatter:
    def __init__(self, grad, acc, core_in, step_in, z_in, out, sems, n_dp, n_seq):
        self.__dict__.update(locals())
        self.bits = n_dp.bit_length() - 1
        self.half = n_seq // 2
        self.high = list(range(self.bits - 1, 0, -1))
        self.orders = (list(range(len(self.high))), list(range(len(self.high)))[::-1])
        self.stages = len(self.high) + 2

    def my(self, dim):
        d, _ = place()
        return lax.rem(lax.div(d, 1 << self.high[dim]), 2)

    def index(self, h, done, flip=None):
        idx = []
        for dim in range(len(self.high)):
            if dim in done:
                idx.append(self.my(dim))
            elif dim == flip:
                idx.append(1 - self.my(dim))
            else:
                idx.append(slice(None))
        return tuple(idx) + (pl.ds(h * self.half, self.half),)

    def core_copies(self):
        d, s = place()
        core = lax.rem(d, 2)
        lead = (slice(None),) * len(self.high)
        send, recv, local = self.sems["core"]
        return (
            pltpu.make_async_copy(self.grad.at[lead + (core,)], self.acc, local),
            remote(
                self.grad.at[lead + (1 - core,)],
                self.core_in,
                send,
                recv,
                xor(d, 1),
                s,
            ),
        )

    def step_copy(self, h, step):
        d, s = place()
        done = self.orders[h][:step]
        dim = self.orders[h][step]
        send, recv = self.sems["step"]
        return remote(
            self.acc.at[self.index(h, done, dim)],
            self.step_in[h][step],
            send.at[h, step],
            recv.at[h, step],
            xor(d, 1 << self.high[dim]),
            s,
        )

    def z_copy(self, off):
        d, s = place()
        to = lax.rem(s + off, self.n_seq)
        send, recv = self.sems["z"]
        idx = tuple(self.my(dim) for dim in range(len(self.high)))
        return remote(
            self.acc.at[idx + (to,)],
            self.z_in.at[off],
            send.at[off],
            recv.at[off],
            d,
            to,
        )

    def start(self):
        for c in self.core_copies():
            c.start()

    def add(self, target, source, lead):
        count = math.prod(lead)

        @pl.loop(0, count)
        def _(k):
            idx = []
            for n in lead[::-1]:
                idx.append(lax.rem(k, n))
                k = lax.div(k, n)
            idx = tuple(idx[::-1])
            target[idx] = target[idx] + source[idx]

    def stage(self, t):
        if t == 0:
            for c in self.core_copies():
                c.wait()
            self.add(self.acc, self.core_in, self.acc.shape[:-2])
        for h in range(2):
            if t:
                if t > len(self.high):
                    continue
                done = self.orders[h][:t]
                self.step_copy(h, t - 1).wait()
                part = self.acc.at[self.index(h, done)]
                source = self.step_in[h][t - 1]
                self.add(part, source, source.shape[:-2])
            if t < len(self.high):
                self.step_copy(h, t).start()
        if t == len(self.high):
            for off in range(1, self.n_seq):
                self.z_copy(off).start()
        if t == len(self.high) + 1:
            _, s = place()
            idx = tuple(self.my(dim) for dim in range(len(self.high)))
            total = self.acc[idx + (s,)].astype(F32)
            for off in range(1, self.n_seq):
                self.z_copy(off).wait()
                total += self.z_in[off].astype(F32)
            self.out[...] = total


def scatter_kernel(n_dp, n_seq, rows, shapes, *refs):
    grads = refs[:4]
    out_row, dtok_row, gmod = refs[4:7]
    outs = refs[7:11]
    out_o, dtok_o, gmod_o = refs[11:14]
    refs = refs[14:]
    high = n_dp.bit_length() - 2
    weights = []
    for w in range(4):
        acc, core_in, z_in = refs[:3]
        steps = (refs[3 : 3 + high], refs[3 + high : 3 + 2 * high])
        refs = refs[3 + 2 * high :]
        weights.append((acc, core_in, steps, z_in))
    (
        row_send,
        row_recv,
        g_send,
        g_recv,
        gd_send,
        gd_recv,
        c_send,
        c_recv,
        c_local,
        s_send,
        s_recv,
        z_send,
        z_recv,
    ) = refs
    d, s = place()
    first = lax.rem(d, 2)
    mine = s - first
    active = jnp.logical_and(mine >= 0, mine < rows)
    greet(n_dp, n_seq)
    parts = [
        GradScatter(
            grads[w],
            weights[w][0],
            weights[w][1],
            weights[w][2],
            weights[w][3],
            outs[w],
            {
                "core": (c_send.at[w], c_recv.at[w], c_local.at[w]),
                "step": (s_send.at[w], s_recv.at[w]),
                "z": (z_send.at[w], z_recv.at[w]),
            },
            n_dp,
            n_seq,
        )
        for w in range(4)
    ]
    for p in parts:
        p.start()

    def group_copy(off):
        return remote(
            gmod,
            gmod_o.at[d, mine],
            g_send.at[off],
            g_recv.at[s],
            d,
            lax.rem(s + off, n_seq),
        )

    @pl.when(active)
    def _():
        pltpu.make_async_copy(gmod, gmod_o.at[d, mine], g_send.at[0]).start()
        for off in range(1, n_seq):
            group_copy(off).start()

    pair = ((out_row, out_o), (dtok_row, dtok_o))

    @pl.when(active)
    def _():
        for k in range(2):
            src, dst = pair[k]
            pltpu.make_async_copy(src.at[s], dst.at[mine], row_send.at[k, 0]).start()
            for off in range(1, n_seq):
                to = lax.rem(s + off, n_seq)
                remote(
                    src.at[to],
                    dst.at[mine],
                    row_send.at[k, off],
                    row_recv.at[k, mine],
                    d,
                    to,
                ).start()

    @pl.when(active)
    def _():
        pltpu.make_async_copy(gmod, gmod_o.at[d, mine], g_send.at[0]).wait()

    for i in range(rows):
        owner = first + i

        @pl.when(owner != s)
        def _():
            remote(
                gmod, gmod_o.at[d, i], g_send.at[0], g_recv.at[owner], d, owner
            ).wait_recv()

    def dp_copy(off):
        return remote(
            gmod_o.at[d], gmod_o.at[d], gd_send.at[off], gd_recv.at[off], xor(d, off), s
        )

    for off in range(1, n_dp):
        dp_copy(off).start()

    stages = parts[0].stages
    for slot in range(stages + 3):
        for w in range(4):
            if 0 <= slot - w < stages:
                parts[w].stage(slot - w)

    for off in range(1, n_dp):
        e = xor(d, off)
        dp_copy(off).wait_send()
        remote(
            gmod_o.at[e], gmod_o.at[e], gd_send.at[off], gd_recv.at[off], e, s
        ).wait_recv()

    @pl.when(active)
    def _():
        for off in range(1, n_seq):
            group_copy(off).wait_send()
        for k in range(2):
            src, dst = pair[k]
            pltpu.make_async_copy(src.at[s], dst.at[mine], row_send.at[k, 0]).wait()
            for off in range(1, n_seq):
                to = lax.rem(s + off, n_seq)
                remote(
                    src.at[to],
                    dst.at[mine],
                    row_send.at[k, off],
                    row_recv.at[k, mine],
                    d,
                    to,
                ).wait_send()

    for k in range(2):
        src, dst = pair[k]
        for i in range(rows):
            owner = first + i

            @pl.when(owner != s)
            def _():
                remote(
                    src.at[0],
                    dst.at[i],
                    row_send.at[k, 0],
                    row_recv.at[k, i],
                    d,
                    owner,
                ).wait_recv()


def scatter(n_dp, n_seq, rows, grads, out_row, dtok_row, gmod):
    dma = pltpu.SemaphoreType.DMA
    struct = jax.ShapeDtypeStruct
    high = n_dp.bit_length() - 2
    half = n_seq // 2
    scratch = []
    outs = []
    lead = (2,) * high
    views = []
    for g in grads:
        slab = g.shape[2:]
        views.append(g.reshape(lead + (2, n_seq) + slab))
        scratch += [
            pltpu.VMEM(lead + (n_seq,) + slab, BF16),
            pltpu.VMEM(lead + (n_seq,) + slab, BF16),
            pltpu.VMEM((n_seq,) + slab, BF16),
        ]
        for _ in range(2):
            for step in range(high):
                scratch.append(pltpu.VMEM((2,) * (high - 1 - step) + (half,) + slab, BF16))
        outs.append(struct(slab, F32))
    length, width = out_row.shape[1:]
    outs += [
        struct((rows, length, width), BF16),
        struct((rows, length, width), BF16),
        struct((n_dp, rows) + gmod.shape, F32),
    ]
    scratch += [
        dma((2, n_seq)),
        dma((2, rows)),
        dma((n_seq,)),
        dma((n_seq,)),
        dma((n_dp,)),
        dma((n_dp,)),
        dma((4,)),
        dma((4,)),
        dma((4,)),
        dma((4, 2, max(high, 1))),
        dma((4, 2, max(high, 1))),
        dma((4, n_seq)),
        dma((4, n_seq)),
    ]
    return pl.pallas_call(
        functools.partial(scatter_kernel, n_dp, n_seq, rows, None),
        out_shape=outs,
        in_specs=[ANY] * 7,
        out_specs=[VMEM] * 4 + [ANY] * 3,
        scratch_shapes=scratch,
        compiler_params=pltpu.CompilerParams(
            collective_id=1, has_side_effects=True, vmem_limit_bytes=VMEM_LIMIT
        ),
    )(*views, out_row, dtok_row, gmod)


def dot(a, b, dims):
    return lax.dot_general(a, b, (dims, ((), ())), preferred_element_type=F32)


def rotary_tables(seq_len):
    half = HEAD_DIM // 2
    freq = np.exp(np.float32(-math.log(10000.0)) * np.arange(half, dtype=np.float32) / np.float32(half))
    angles = np.arange(seq_len, dtype=np.float32)[:, None] * freq.astype(np.float32)[None, :]
    cos = np.tile(np.cos(angles), (1, 4)).astype(np.float32)
    sin = np.sin(angles)
    sin = np.concatenate([-sin, sin, -sin, sin], 1).astype(np.float32)
    return jnp.asarray(cos), jnp.asarray(sin)


def swap_halves(x):
    quarter = HEAD_DIM // 2
    lane = lax.broadcasted_iota(jnp.int32, x.shape, 1)
    return jnp.where(
        lax.rem(lane, HEAD_DIM) < quarter,
        pltpu.roll(x, 128 - quarter, axis=1),
        pltpu.roll(x, quarter, axis=1),
    )


def qkv_kernel(tok, mod, w, cos, sin, normed_o, packed_o):
    x = tok[...].astype(F32)
    mean = jnp.mean(x, -1, keepdims=True)
    centred = x - mean
    var = jnp.mean(centred * centred, -1, keepdims=True)
    z = centred * lax.rsqrt(var + EPSILON)
    gain = mod[6:7, :] * (1.0 + mod[1:2, :])
    normed = (z * gain + mod[0:1, :]).astype(BF16)
    normed_o[...] = normed
    width = x.shape[1]
    for c in range(3 * width // 256):
        y = dot(normed, w[:, c * 256 : (c + 1) * 256], ((1,), (0,)))
        for j in range(2):
            col = c * 256 + j * 128
            p = y[:, j * 128 : (j + 1) * 128]
            if col < 2 * width:
                p = p * cos[...] + swap_halves(p) * sin[...]
            if col < width:
                p = p * (1.0 / math.sqrt(HEAD_DIM))
            packed_o[:, col : col + 128] = p.astype(BF16)


def qkv_call(tok, mod, w, cos, sin):
    seq_len, width = tok.shape
    block = 256
    return pl.pallas_call(
        qkv_kernel,
        grid=(seq_len // block,),
        in_specs=[
            pl.BlockSpec((block, width), lambda i: (i, 0)),
            pl.BlockSpec((8, width), lambda i: (0, 0)),
            pl.BlockSpec((width, 3 * width), lambda i: (0, 0)),
            pl.BlockSpec((block, 128), lambda i: (i, 0)),
            pl.BlockSpec((block, 128), lambda i: (i, 0)),
        ],
        out_specs=[
            pl.BlockSpec((block, width), lambda i: (i, 0)),
            pl.BlockSpec((block, 3 * width), lambda i: (i, 0)),
        ],
        out_shape=[
            jax.ShapeDtypeStruct((seq_len, width), BF16),
            jax.ShapeDtypeStruct((seq_len, 3 * width), BF16),
        ],
        compiler_params=pltpu.CompilerParams(vmem_limit_bytes=VMEM_LIMIT),
    )(tok, mod, w, cos, sin)


def head_mask(x, j):
    lane = lax.broadcasted_iota(jnp.int32, x.shape, 1)
    return jnp.where(lax.div(lane, HEAD_DIM) == j, x, jnp.zeros_like(x))


def attend_kernel(q, k, v, seg_col, seg_row, out, lse_o):
    seq_len = q.shape[0]
    block = 256
    keys = k[...]
    values = v[...]
    for i in range(seq_len // block):
        rows = pl.ds(i * block, block)
        bias = jnp.where(seg_col[rows, 0:1] == seg_row[0:1, :], 0.0, MASK_FILL)
        qb = q[rows, :]
        both = []
        stats = []
        for j in range(2):
            sc = dot(head_mask(qb, j), keys, ((1,), (1,))) + bias
            top = jnp.max(sc, -1, keepdims=True)
            e = jnp.exp(sc - top)
            total = jnp.sum(e, -1, keepdims=True)
            o = dot(e.astype(BF16), values, ((1,), (0,)))
            both.append(o / total)
            stats.append(top + jnp.log(total))
        lane = lax.broadcasted_iota(jnp.int32, both[0].shape, 1)
        out[rows, :] = jnp.where(lane < HEAD_DIM, both[0], both[1]).astype(BF16)
        lse_o[rows, :] = jnp.where(lane < HEAD_DIM, stats[0], stats[1])


def attend_call(packed, seg_col, seg_row):
    seq_len, width3 = packed.shape
    width = width3 // 3
    pairs = width // 128
    return pl.pallas_call(
        attend_kernel,
        grid=(pairs,),
        in_specs=[
            pl.BlockSpec((seq_len, 128), lambda i: (0, i)),
            pl.BlockSpec((seq_len, 128), lambda i: (0, i + pairs)),
            pl.BlockSpec((seq_len, 128), lambda i: (0, i + 2 * pairs)),
            pl.BlockSpec((seq_len, 128), lambda i: (0, 0)),
            pl.BlockSpec((8, seq_len), lambda i: (0, 0)),
        ],
        out_specs=[
            pl.BlockSpec((seq_len, 128), lambda i: (0, i)),
            pl.BlockSpec((seq_len, 128), lambda i: (0, i)),
        ],
        out_shape=[
            jax.ShapeDtypeStruct((seq_len, width), BF16),
            jax.ShapeDtypeStruct((seq_len, width), F32),
        ],
        compiler_params=pltpu.CompilerParams(vmem_limit_bytes=VMEM_LIMIT),
    )(packed, packed, packed, seg_col, seg_row)


def attend_back_kernel(
    q, k, v, o, do, lse, seg_col, seg_row, cos, sin, dq_o, dk_o, dv_o, dq_acc
):
    seq_len = q.shape[0]
    block = 256
    grads = do[...]
    inner = jnp.transpose(grads.astype(F32) * o[...].astype(F32))
    lse_t = jnp.transpose(lse[...])
    queries = q[...]
    scale = 1.0 / math.sqrt(HEAD_DIM)
    inners, lses, qs, gs = [], [], [], []
    for j in range(2):
        inners.append(
            jnp.sum(inner[j * HEAD_DIM : (j + 1) * HEAD_DIM], 0, keepdims=True)
        )
        lses.append(lse_t[j * HEAD_DIM : j * HEAD_DIM + 1])
        qs.append(head_mask(queries, j))
        gs.append(head_mask(grads, j))
    for i in range(seq_len // block):
        rows = pl.ds(i * block, block)
        bias = jnp.where(seg_col[rows, 0:1] == seg_row[0:1, :], 0.0, MASK_FILL)
        kb = k[rows, :]
        vb = v[rows, :]
        dk = None
        for j in range(2):
            sc = dot(kb, qs[j], ((1,), (1,))) + bias
            p = jnp.exp(sc - lses[j])
            dp = dot(vb, gs[j], ((1,), (1,)))
            ds = (p * (dp - inners[j])).astype(BF16)
            dv_j = dot(p.astype(BF16), gs[j], ((1,), (0,)))
            dk_j = dot(ds, qs[j], ((1,), (0,)))
            dq_j = dot(ds, head_mask(kb, j), ((0,), (0,)))
            if j == 0:
                dv, dk, dq = dv_j, dk_j, dq_j
            else:
                dv, dk, dq = dv + dv_j, dk + dk_j, dq + dq_j
        if i == 0:
            dq_acc[...] = dq
        else:
            dq_acc[...] += dq
        dv_o[rows, :] = dv.astype(BF16)
        dk_o[rows, :] = (dk * cos[rows, :] + swap_halves(dk * sin[rows, :]) * 1.0).astype(BF16)
    dq = dq_acc[...] * scale
    dq_o[...] = (dq * cos[...] + swap_halves(dq * sin[...])).astype(BF16)


def attend_back_call(packed, mixed, grad_mixed, lse, seg_col, seg_row, cos, sin):
    seq_len, width3 = packed.shape
    width = width3 // 3
    pairs = width // 128
    pair = pl.BlockSpec((seq_len, 128), lambda i: (0, i))
    whole = pl.BlockSpec((seq_len, 128), lambda i: (0, 0))
    return pl.pallas_call(
        attend_back_kernel,
        grid=(pairs,),
        in_specs=[
            pair,
            pl.BlockSpec((seq_len, 128), lambda i: (0, i + pairs)),
            pl.BlockSpec((seq_len, 128), lambda i: (0, i + 2 * pairs)),
            pair,
            pair,
            pair,
            whole,
            pl.BlockSpec((8, seq_len), lambda i: (0, 0)),
            whole,
            whole,
        ],
        out_specs=[pair] * 3,
        out_shape=[jax.ShapeDtypeStruct((seq_len, width), BF16)] * 3,
        scratch_shapes=[pltpu.VMEM((seq_len, 128), F32)],
        compiler_params=pltpu.CompilerParams(vmem_limit_bytes=VMEM_LIMIT),
    )(packed, packed, packed, mixed, grad_mixed, lse, seg_col, seg_row, cos, sin)


def time_embed(step_ids, model_dim):
    half_dim = model_dim // 2
    frequency = jnp.exp(-math.log(10000.0) * jnp.arange(half_dim, dtype=jnp.float32) / half_dim)
    angles = step_ids.astype(jnp.float32)[:, None] * frequency[None, :]
    return jnp.concatenate([jnp.cos(angles), jnp.sin(angles)], axis=-1)


def modulate(inputs, norm_gain, mod_scale, mod_shift):
    average = jnp.mean(inputs, -1, keepdims=True)
    centred = inputs - average
    variance = jnp.mean(centred * centred, -1, keepdims=True)
    return centred * lax.rsqrt(variance + EPSILON) * norm_gain * (1.0 + mod_scale) + mod_shift


def matmul(a, b, spec):
    return jnp.einsum(spec, a, b, preferred_element_type=F32)


def placed_at(vector, index, length):
    whole = jnp.zeros((length,), F32)
    return lax.dynamic_update_slice(whole, vector.astype(F32), (index * vector.shape[0],))


def shards(
    n_dp,
    n_seq,
    tokens,
    segments,
    timesteps,
    w_mod,
    b_mod,
    gain_attn,
    w_qkv,
    w_out,
    gain_mlp,
    w_up,
    w_down,
    cotangent,
):
    rows, length, width = tokens.shape
    seq_len = length * n_seq
    hidden = w_up.shape[1]
    d, s = place()
    me = d * n_seq + s
    depth = w_mod.shape[0]
    cos, sin = rotary_tables(seq_len)

    steps = lax.all_gather(timesteps, "dp", axis=0, tiled=True)
    embedding = lax.dynamic_slice_in_dim(
        time_embed(steps, width).astype(BF16), me * depth, depth, 1
    )
    part = matmul(embedding, w_mod, "rk,kn->rn") + placed_at(b_mod, me, 6 * width)
    gains = jnp.concatenate(
        [placed_at(gain_attn, me, width), placed_at(gain_mlp, me, width)]
    )
    part = jnp.concatenate([part, jnp.broadcast_to(gains, (part.shape[0], 2 * width))], 1)
    part = part.reshape(n_dp, rows, 8, width)
    seg = jnp.broadcast_to(segments[:, None, :], (rows, 8, length))

    tok, cot, seg, mod, wq, wo, wu, wd = gather(
        n_dp, n_seq, tokens, cotangent, seg, part, (w_qkv, w_out, w_up, w_down)
    )
    tok = tok.reshape(seq_len, width)
    cot = cot.reshape(seq_len, width).astype(F32)
    seg_row = seg.transpose(1, 0, 2).reshape(8, seq_len)
    seg_col = jnp.broadcast_to(seg_row[0][:, None], (seq_len, 128))
    wq = wq.reshape(width, 3 * width)
    wo = wo.reshape(width, width)
    wu = wu.reshape(width, hidden)
    wd = wd.reshape(hidden, width)
    shift_a, scale_a, gate_a, shift_m, scale_m, gate_m, gain_a, gain_m = (
        mod[j : j + 1] for j in range(8)
    )

    normed_a, packed = qkv_call(tok, mod, wq, cos, sin)
    mixed, lse = attend_call(packed, seg_col, seg_row)

    stream = tok.astype(F32)
    attn_out = matmul(mixed, wo, "td,de->te")
    middle = stream + gate_a * attn_out
    normed_m, norm_back_m = jax.vjp(modulate, middle, gain_m, scale_m, shift_m)
    normed_m = normed_m.astype(BF16)
    up_proj = matmul(normed_m, wu, "td,df->tf")
    activated, gelu_back = jax.vjp(jax.nn.gelu, up_proj)
    activated = activated.astype(BF16)
    mlp_out = matmul(activated, wd, "tf,fd->td")
    output = (middle + gate_m * mlp_out).astype(BF16)

    grad_mlp = (cot * gate_m).astype(BF16)
    grad_gate_m = jnp.sum(cot * mlp_out, 0, keepdims=True)
    grad_down = matmul(activated, grad_mlp, "tf,td->fd").astype(BF16)
    grad_act = matmul(grad_mlp, wd, "td,fd->tf")
    grad_up = gelu_back(grad_act)[0].astype(BF16)
    grad_wup = matmul(normed_m, grad_up, "td,tf->df").astype(BF16)
    grad_hm = matmul(grad_up, wu, "tf,df->td")
    grad_mid_norm, grad_gain_m, grad_scale_m, grad_shift_m = norm_back_m(grad_hm)
    grad_mid = cot + grad_mid_norm
    grad_gate_a = jnp.sum(grad_mid * attn_out, 0, keepdims=True)
    grad_attn = (grad_mid * gate_a).astype(BF16)
    grad_wout = matmul(mixed, grad_attn, "td,te->de").astype(BF16)
    grad_mixed = matmul(grad_attn, wo, "te,de->td").astype(BF16)

    dq, dk, dv = attend_back_call(
        packed, mixed, grad_mixed, lse, seg_col, seg_row, cos, sin
    )
    grad_qkv = jnp.concatenate([dq, dk, dv], 1)
    grad_wqkv = matmul(normed_a, grad_qkv, "td,te->de").astype(BF16)
    grad_ha = matmul(grad_qkv, wq, "te,de->td")
    _, norm_back_a = jax.vjp(modulate, stream, gain_a, scale_a, shift_a)
    grad_in_norm, grad_gain_a, grad_scale_a, grad_shift_a = norm_back_a(grad_ha)
    grad_input = (grad_mid + grad_in_norm).astype(BF16)
    gmod = jnp.concatenate(
        [
            grad_shift_a,
            grad_scale_a,
            grad_gate_a,
            grad_shift_m,
            grad_scale_m,
            grad_gate_m,
            grad_gain_a,
            grad_gain_m,
        ],
        0,
    )

    def cut(g, shard):
        return g.reshape((n_dp, n_seq) + shard.shape)

    g_wqkv, g_wout, g_wup, g_wdown, out, d_tok, gmods = scatter(
        n_dp,
        n_seq,
        rows,
        (
            cut(grad_wqkv, w_qkv),
            cut(grad_wout, w_out),
            cut(grad_wup, w_up),
            cut(grad_down, w_down),
        ),
        output.reshape(n_seq, length, width),
        grad_input.reshape(n_seq, length, width),
        gmod,
    )
    gmods = gmods.reshape(n_dp * rows, 8 * width)
    g_w_mod = jnp.dot(
        embedding.astype(F32).T,
        gmods[:, : 6 * width],
        precision=lax.Precision.HIGHEST,
        preferred_element_type=F32,
    )
    summed = jnp.sum(gmods, 0)

    def own_part(vector, n):
        return lax.dynamic_slice_in_dim(vector, me * n, n, 0)

    return (
        out,
        d_tok,
        g_w_mod,
        own_part(summed[: 6 * width], b_mod.shape[0]),
        own_part(summed[6 * width : 7 * width], gain_attn.shape[0]),
        g_wqkv,
        g_wout,
        own_part(summed[7 * width :], gain_mlp.shape[0]),
        g_wup,
        g_wdown,
    )


def solution(mesh):
    both = P(("dp", "seq"))
    wide = P(("dp", "seq"), None)
    tokens = P("dp", "seq", None)
    return jax.shard_map(
        functools.partial(shards, mesh.shape["dp"], mesh.shape["seq"]),
        mesh=mesh,
        in_specs=(
            tokens,
            P("dp", "seq"),
            P("dp"),
            wide,
            both,
            both,
            wide,
            wide,
            both,
            wide,
            wide,
            tokens,
        ),
        out_specs=(tokens, tokens, wide, both, both, wide, wide, both, wide, wide),
        check_vma=False,
    )
```

time: 1280 us -> 442 us (0.35)
  waiting for transfers between devices: 457 us -> 0 us
  blocking collectives: 381 us -> 8.01 us
  Pallas kernels: 0 us -> 307 us
  matrix products: 209 us -> 87.5 us
  local copies, waits for them, and re-layouts: 106 us -> 17.9 us
  other arithmetic: 79.5 us -> 15.7 us
  starting transfers between devices: 25.2 us -> 0 us
  between operations: 15.5 us -> 1.94 us
    pallas_call x0 -> x5, Pallas kernels: none -> 307 us  [the longest x1 117 us: gather(): pl.pallas_call(functools.partial(gather_kernel, n_dp, n_seq, rows), out_s...]
    reduce_scatter x5 -> x0, waiting for transfers between devices: 294 us -> none  [the longest x1 168 us: shards(): lax.psum_scatter(grad_wmod, ('dp', 'seq'), scatter_dimension=0, tiled=True)]
    all_to_all x1 -> x0, blocking collectives: 185 us -> none  [shards(): lax.all_to_all(grad_packed, 'seq', split_axis=1, concat_axis=3, tiled=True)]
    all_gather x1 -> x0, blocking collectives: 116 us -> none  [shards(): whole_docs = lax.all_gather(segments, 'seq', axis=1, tiled=True)]
    dot_general x40 -> x13, matrix products: 186 us -> 87.5 us  [the longest x12 86.3 us: matmul(): return jnp.einsum(spec, a, b, preferred_element_type=F32)]
    all_gather x5 -> x0, waiting for transfers between devices: 83.1 us -> none  [the longest x1 68.1 us: shards(): lax.all_gather(w_mod, ('dp', 'seq'), axis=0, tiled=True)]
    all_to_all x4 -> x0, waiting for transfers between devices: 77.4 us -> none  [the longest x2 49.9 us: shards(): lax.all_to_all(heads_out, 'seq', split_axis=1, concat_axis=2, tiled=True)]
    unnamed x2 -> x1, blocking collectives: 80.5 us -> 8.01 us
  transfers between devices with their start and end apart: 14 -> 0, of which waited for: 8 -> 0; matrix products, arithmetic and copies ran while one was open for 27% -> 0% of each run, Pallas kernels for 0% -> 0%
where the time goes in v1:
time: 442 us; the launch traced here: 438 us
  Pallas kernels  307 us (69%)
  matrix products  87.5 us (20%)
  local copies, waits for them, and re-layouts  17.9 us (4%)
  other arithmetic  15.7 us (4%)
  blocking collectives  8.01 us (2%)
    pallas_call x1, Pallas kernels, gather(): pl.pallas_call(functools.partial(gather_kernel, n_dp, n_seq, rows), out_s...  117 us
    pallas_call x1, Pallas kernels, scatter(): pl.pallas_call(functools.partial(scatter_kernel, n_dp, n_seq, rows, None)...  110 us
    dot_general x12, matrix products, matmul(): return jnp.einsum(spec, a, b, preferred_element_type=F32)  86.3 us
    pallas_call x1, Pallas kernels, attend_back_call(): pl.pallas_call(attend_back_kernel, grid=(pairs,), in_specs=[pair, pl.Bloc...  41.9 us
    pallas_call x1, Pallas kernels, attend_call(): pl.pallas_call(attend_kernel, grid=(pairs,), in_specs=[pl.BlockSpec((seq_...  29.2 us
    unnamed x65, local copies, waits for them, and re-layouts  12.7 us
    pallas_call x1, Pallas kernels, qkv_call(): pl.pallas_call(qkv_kernel, grid=(seq_len // block,), in_specs=[pl.BlockSp...  9.22 us

profile of v1, /device:TPU:24, one launch (start us, length us, event | category | flops | bytes accessed | tf_op | source)
XLA Modules:
  0.0 438.1 jit_solution(4340890758422724075)
XLA Ops:
  0.6 0.0 copy-start
  0.7 1.3 dynamic-slice.2
  2.6 0.9 dynamic-update-slice
  3.5 8.0 %all-reduce = s32[24]{0:T(128)S(1)} all-reduce(s32[24]{0:T(128)S(1)} %dynamic-update-slice), channel_id=1, replica_groups=mesh['dp'=8,'seq'=4] {'dp'}, use_global_device_ids=true, to_apply=%add | all-reduce | flops 24 | bytes 192
  11.5 0.8 convert_dynamic-update-slice_fusion.1
  12.3 0.7 convert_dynamic-update-slice_fusion.2
  13.0 0.8 convert_dynamic-update-slice_fusion
  13.8 1.3 broadcast_in_dim.20.refs_2_
  15.1 0.2 fusion.24
  15.3 0.3 convolution_add_fusion
  15.7 1.0 copy.24
  16.7 116.7 %shard_map.213 = (bf16[4,256,768]{2,1,0:T(8,128)(2,1)}, bf16[4,256,768]{2,1,0:T(8,128)(2,1)}, s32[4,8,256]{2,1,0:T(8,128)}, f32[8,768]{1,0:T(8,128)}, bf16[8,4,2...) custom-call(bf16[3,256,768]{2,1,0:T(8,128)(2,1)} %refs_0_.1, ...), custom_call_target="tpu_custom_call" | custom-call | tf_op jit(solution)/shard_map/pallas_call | solution.py:350
  133.4 0.9 slice.55
  134.3 1.7 convert_reduce_fusion
  136.0 2.0 fusion.17
  138.0 0.1 add_reduce_fusion
  138.1 1.0 broadcast_in_dim.45.seg_col
  139.1 0.3 fusion.18
  139.4 9.2 %shard_map.214 = (bf16[1024,768]{1,0:T(8,128)(2,1)}, bf16[1024,2304]{1,0:T(8,128)(2,1)}) custom-call(bf16[1024,768]{1,0:T(8,128)(2,1)} %bitcast.70, f32[8,768]{1,0:T(8,128)} %get-tuple-element.33.mod, bf16[768,2304]{1,0:T(8,128)(2,1)} %bitcast.75, f32[1024,128]{1,0:T(8,128)} %constant.65.clone.cos, f32[1024,128]{1,0:T(8,128)} %constant.66.clone.sin), custom_call_target="tpu_custom_call" | custom-call | tf_op jit(solution)/shard_map/pallas_call | solution.py:753
  148.6 29.2 %shard_map.215 = (bf16[1024,768]{1,0:T(8,128)(2,1)}, f32[1024,768]{1,0:T(8,128)}) custom-call(bf16[1024,2304]{1,0:T(8,128)(2,1)} %get-tuple-element.36.q.k.v, bf16[1024,2304]{1,0:T(8,128)(2,1)} %get-tuple-element.36.q.k.v, bf16[1024,2304]{1,0:T(8,128)(2,1)} %get-tuple-element.36.q.k.v, s32[1024,128]{1,0:T(8,128)} %broadcast_in_dim.45.seg_col, s32[8,1024]{1,0:T(8,128)} %bitcast.87), custom_call_target="tpu_custom_call" | custom-call | tf_op jit(solution)/shard_map/pallas_call | solution.py:808
  177.8 0.0 copy-done.11
  177.9 0.0 slice-start.3
  177.9 3.1 fusion.36
  181.0 0.0 slice-start
  181.0 0.5 multiply_reduce_fusion.4
  181.5 0.0 slice-start.1
  181.5 8.3 %fusion.33 = f32[1024,3072]{1,0:T(8,128)} fusion(bf16[768,3072]{1,0:T(8,128)(2,1)S(1)} %bitcast.102, f32[1024,768]{1,0:T(8,128)S(1)} %get-tuple-element.74, f32[768]{0:T(1024)S(1)} %get-tuple-element.64, f32[768]{0:T(1024)S(1)} %get-tuple-element.65, f32[768]{0:T(1024)S(1)} %get-tuple-element.66, f32[1024]{0:T(1024)S(1)} %fusion.26, ...), kind=kOutput, calls=%fused_computation.89 | convolution fusion | flops 4836556800 | bytes 20464640 | tf_op jit(solution)/shard_map/td,df->tf/dot_general | solution.py:919
  189.8 15.5 %fusion.6 = bf16[1024,3072]{1,0:T(8,128)(2,1)} fusion(f32[1024,3072]{1,0:T(8,128)} %fusion.33, bf16[1024,768]{1,0:T(8,128)(2,1)S(1)} %bitcast.82, bf16[3072,768]{1,0:T(8,128)(2,1)S(1)} %bitcast.98), kind=kOutput, calls=%fused_computation.8 | convolution fusion | flops 4894752768 | bytes 25165824 | tf_op jit(solution)/shard_map/td,fd->tf/dot_general | solution.py:919
  205.4 10.7 %multiply_reduce_fusion = (f32[768]{0:T(1024)S(1)}, f32[1024]{0:T(1024)S(1)}, f32[768]{0:T(1024)S(1)}, f32[768]{0:T(1024)S(1)}, f32[1024,768]{1,0:T(8,128)}) fusion(f32[1024,768]{1,0:T(8,128)S(1)} %get-tuple-element.74, f32[768]{0:T(1024)S(1)} %get-tuple-element.65, f32[1024]{0:T(1024)S(1)} %fusion.26, f32[1024]{0:T(1024)S(1)} %broadcast_multiply_fusion.1, ...), kind=kOutput, calls=%fused_computation.38 | convolution fusion | flops 4841271296 | bytes 17329152 | tf_op jit(solution)/shard_map/tf,df->td/dot_general | solution.py:919
  216.1 0.0 copy-done.20
  216.1 7.5 %convolution_convert_fusion.1 = bf16[768,3072]{1,0:T(8,128)(2,1)} fusion(bf16[1024,3072]{1,0:T(8,128)(2,1)S(1)} %copy-done.20, f32[1024,768]{1,0:T(8,128)S(1)} %get-tuple-element.74, f32[768]{0:T(1024)S(1)} %get-tuple-element.64, f32[768]{0:T(1024)S(1)} %get-tuple-element.65, f32[768]{0:T(1024)S(1)} %get-tuple-element.66, f32[1024]{0:T(1024)S(1)} %fusion.26, ...), kind=kOutput, calls=%fused_computation.12 | convolution fusion | flops 4838916096 | bytes 14173184 | tf_op jit(solution)/shard_map/td,tf->df/dot_general | solution.py:919
  223.6 14.4 %fusion.20 = (f32[768]{0:T(1024)S(1)}, bf16[1024,768]{1,0:T(8,128)(2,1)}, f32[1024]{0:T(1024)S(1)}, f32[1024,768]{1,0:T(8,128)S(1)}, bf16[1024,768]{1,0:T(8,128)(2,1)S(1)}) fusion(bf16[4,256,768]{2,1,0:T(8,128)(2,1)S(1)} %copy-done.5, f32[1024,768]{1,0:T(8,128)S(1)} %get-tuple-element.74, f32[768]{0:T(1024)S(1)} %get-tuple-element.68, ...), kind=kOutput, calls=%fused_computation.37 | convolution fusion | flops 4872730624 | bytes 31485952 | tf_op jit(solution)/shard_map/tf,fd->td/dot_general | solution.py:919
  238.1 11.6 %convolution_convert_fusion = bf16[3072,768]{1,0:T(8,128)(2,1)} fusion(bf16[1024,768]{1,0:T(8,128)(2,1)S(1)} %get-tuple-element.79, f32[1024,3072]{1,0:T(8,128)} %fusion.33), kind=kOutput, calls=%fused_computation.11 | convolution fusion | flops 4862509056 | bytes 18874368 | tf_op jit(solution)/shard_map/tf,td->fd/dot_general | solution.py:919
  249.8 0.6 multiply_reduce_fusion.2
  250.4 2.6 convolution_convert_fusion.3.do
  253.0 41.9 %shard_map.216 = (bf16[1024,768]{1,0:T(8,128)(2,1)}, bf16[1024,768]{1,0:T(8,128)(2,1)}, bf16[1024,768]{1,0:T(8,128)(2,1)}) custom-call(bf16[1024,2304]{1,0:T(8,128)(2,1)} %get-tuple-element.36.q.k.v, bf16[1024,2304]{1,0:T(8,128)(2,1)} %get-tuple-element.36.q.k.v, bf16[1024,2304]{1,0:T(8,128)(2,1)} %get-tuple-element.36.q.k.v, ...), custom_call_target="tpu_custom_call" | custom-call | tf_op jit(solution)/shard_map/pallas_call | solution.py:882
  295.0 2.5 convolution_convert_fusion.4
  297.5 0.1 constant_dynamic-update-slice_fusion.2
  297.6 1.3 copy-done.9
  298.9 0.1 constant_dynamic-update-slice_fusion.1
  299.0 0.4 copy-done.8
  299.4 0.1 constant_dynamic-update-slice_fusion
  299.5 1.5 copy-done.7
  301.0 4.1 fusion.15
  305.2 5.5 %convolution_convert_fusion.2 = bf16[768,2304]{1,0:T(8,128)(2,1)} fusion(bf16[1024,768]{1,0:T(8,128)(2,1)S(1)} %copy-done.19, bf16[1024,2304]{1,0:T(8,128)(2,1)S(1)} %constant_dynamic-update-slice_fusion), kind=kOutput, calls=%fused_computation.13 | convolution fusion | flops 3625648128 | bytes 9830400 | tf_op jit(solution)/shard_map/td,te->de/dot_general | solution.py:919
  310.7 2.3 fusion.14
  313.0 0.7 concatenate.20.refs_6_
  313.7 4.4 %add_convert_fusion = bf16[1024,768]{1,0:T(8,128)(2,1)} fusion(f32[1024,768]{1,0:T(8,128)} %copy-done.3, f32[1024]{0:T(1024)S(1)} %negate_multiply_fusion, f32[1024]{0:T(1024)S(1)} %get-tuple-element.82, f32[1024]{0:T(1024)S(1)} %bitcast.92, bf16[4,256,768]{2,1,0:T(8,128)(2,1)S(1)} %copy-done.2, f32[1024]{0:T(1024)S(1)} %get-tuple-element.83, ...), kind=kLoop, calls=%fused_computation.41 | loop fusion | flops 8650752 | bytes 9459712 | tf_op jit(solution)/shard_map/convert_element_type | solution.py:1014
  318.1 109.9 %shard_map.217 = (f32[24,2304]{1,0:T(8,128)}, f32[24,768]{1,0:T(8,128)}, f32[24,3072]{1,0:T(8,128)}, f32[96,768]{1,0:T(8,128)}, bf16[3,256,768]{2,1,0:T(8,128)(2...) custom-call(bf16[2,2,2,4,24,2304]{5,4,3,2,1,0:T(8,128)(2,1)} %bitcast.74, ...), custom_call_target="tpu_custom_call" | custom-call | tf_op jit(solution)/shard_map/pallas_call | solution.py:692
  428.0 0.0 copy-start.13
  428.0 0.0 copy-start.12
  428.0 1.3 reduce_sum.185
  429.3 0.6 fusion.27
  429.9 0.6 dynamic_slice.17
  430.5 1.3 copy.27
  431.8 0.0 copy-start.1
  431.8 1.2 fusion.21
  433.1 1.0 copy.41
  434.1 1.0 copy.42
  435.1 0.0 copy-done.16
  435.1 0.7 copy.43
  435.8 0.6 copy.44
  436.4 0.7 copy.45
  437.1 0.7 copy.46
  (67 shorter events, 0.3 us)
Async XLA Ops:
  0.6 14.7 %copy-start = (bf16[24,4608]{1,0:T(8,128)(2,1)S(1)}, bf16[24,4608]{1,0:T(8,128)(2,1)}, u32[]{:S(2)}) copy-start(bf16[24,4608]{1,0:T(8,128)(2,1)} %param.17) | copy-start | bytes 663556
  133.4 4.6 %copy-start.17 = (f32[8,768]{1,0:T(8,128)S(1)}, f32[8,768]{1,0:T(8,128)}, u32[]{:S(2)}) copy-start(f32[8,768]{1,0:T(8,128)} %get-tuple-element.33.mod) | copy-start | bytes 73732
  133.4 5.7 %copy-start.5 = (bf16[4,256,768]{2,1,0:T(8,128)(2,1)S(1)}, bf16[4,256,768]{2,1,0:T(8,128)(2,1)}, u32[]{:S(2)}) copy-start(bf16[4,256,768]{2,1,0:T(8,128)(2,1)} %get-tuple-element.39) | copy-start | bytes 4718596
  148.6 29.2 %copy-start.2 = (bf16[4,256,768]{2,1,0:T(8,128)(2,1)S(1)}, bf16[4,256,768]{2,1,0:T(8,128)(2,1)}, u32[]{:S(2)}) copy-start(bf16[4,256,768]{2,1,0:T(8,128)(2,1)} %get-tuple-element.32) | copy-start | bytes 4718596
  148.6 29.2 %copy-start.11 = (bf16[8,4,24,768]{3,2,1,0:T(8,128)(2,1)S(1)}, bf16[8,4,24,768]{3,2,1,0:T(8,128)(2,1)}, u32[]{:S(2)}) copy-start(bf16[8,4,24,768]{3,2,1,0:T(8,128)(2,1)} %get-tuple-element.41) | copy-start | bytes 3538948
  177.8 3.6 slice-start.2
  177.9 3.6 slice-start.3
  181.0 8.9 %slice-start = ((s8[4718592]{0:T(1024)(128)(4,1)}), s8[4194304]{0:T(1024)(128)(4,1)S(1)}, s32[]{:S(2)}) async-start(s8[4718592]{0:T(1024)(128)(4,1)} %bitcast.96), calls=%async_computation | async-start | bytes 8388608
  181.5 8.3 %slice-start.1 = ((s8[4718592]{0:T(1024)(128)(4,1)}), s8[524288]{0:T(1024)(128)(4,1)S(1)}, s32[]{:S(2)}) async-start(s8[4718592]{0:T(1024)(128)(4,1)} %bitcast.96), calls=%async_computation.1 | async-start | bytes 1048576
  205.4 10.7 %copy-start.20 = (bf16[1024,3072]{1,0:T(8,128)(2,1)S(1)}, bf16[1024,3072]{1,0:T(8,128)(2,1)}, u32[]{:S(2)}) copy-start(bf16[1024,3072]{1,0:T(8,128)(2,1)} %fusion.6) | copy-start | bytes 18874372
  250.4 44.6 %copy-start.3 = (f32[1024,768]{1,0:T(8,128)}, f32[1024,768]{1,0:T(8,128)S(1)}, u32[]{:S(2)}) copy-start(f32[1024,768]{1,0:T(8,128)S(1)} %get-tuple-element.70) | copy-start | bytes 9437188
  253.0 42.0 %copy-start.6 = (bf16[1024,768]{1,0:T(8,128)(2,1)S(1)}, bf16[1024,768]{1,0:T(8,128)(2,1)}, u32[]{:S(2)}) copy-start(bf16[1024,768]{1,0:T(8,128)(2,1)} %get-tuple-element.38.o) | copy-start | bytes 4718596
  295.0 2.5 copy-start.10
  297.5 1.4 copy-start.9
  297.5 1.9 copy-start.8
  298.9 2.1 copy-start.7
  301.0 4.1 copy-start.19
  305.2 5.5 %copy-start.4 = (f32[1024,768]{1,0:T(8,128)}, f32[1024,768]{1,0:T(8,128)S(1)}, u32[]{:S(2)}) copy-start(f32[1024,768]{1,0:T(8,128)S(1)} %get-tuple-element.91) | copy-start | bytes 9437188
  428.0 5.1 %copy-start.13 = (bf16[3,256,768]{2,1,0:T(8,128)(2,1)S(1)}, bf16[3,256,768]{2,1,0:T(8,128)(2,1)}, u32[]{:S(2)}) copy-start(bf16[3,256,768]{2,1,0:T(8,128)(2,1)} %get-tuple-element.104) | copy-start | bytes 3538948
  428.0 6.1 %copy-start.12 = (bf16[3,256,768]{2,1,0:T(8,128)(2,1)S(1)}, bf16[3,256,768]{2,1,0:T(8,128)(2,1)}, u32[]{:S(2)}) copy-start(bf16[3,256,768]{2,1,0:T(8,128)(2,1)} %get-tuple-element.105) | copy-start | bytes 3538948
  430.5 4.6 %copy-start.16 = (f32[24,2304]{1,0:T(8,128)S(1)}, f32[24,2304]{1,0:T(8,128)}, u32[]{:S(2)}) copy-start(f32[24,2304]{1,0:T(8,128)} %get-tuple-element.109) | copy-start | bytes 663556
  431.8 4.0 copy-start.18
  431.8 4.6 %copy-start.15 = (f32[24,3072]{1,0:T(8,128)S(1)}, f32[24,3072]{1,0:T(8,128)}, u32[]{:S(2)}) copy-start(f32[24,3072]{1,0:T(8,128)} %get-tuple-element.112) | copy-start | bytes 884740
  431.8 6.0 %copy-start.1 = (bf16[24,4608]{1,0:T(8,128)(2,1)S(1)}, bf16[24,4608]{1,0:T(8,128)(2,1)}, u32[]{:S(2)}) copy-start(bf16[24,4608]{1,0:T(8,128)(2,1)} %param.17) | copy-start | bytes 663556
  433.1 4.1 copy-start.14

commit v2 on v1

v2 whole, which is shorter than its diff:
```python
import functools
import math

import jax
import jax.numpy as jnp
import numpy as np
from jax import lax
from jax.experimental import pallas as pl
from jax.experimental.pallas import tpu as pltpu
from jax.sharding import PartitionSpec as P

HEAD_DIM = 64
EPSILON = 1e-06
MASK_FILL = -1e30
MESH = pl.DeviceIdType.MESH
BF16 = jnp.bfloat16
F32 = jnp.float32
ANY = pl.BlockSpec(memory_space=pl.ANY)
VMEM = pl.BlockSpec(memory_space=pltpu.VMEM)
VMEM_LIMIT = 60 * 2**20
LOG2E = math.log2(math.e)


def place():
    return lax.axis_index("dp"), lax.axis_index("seq")


def xor(index, bits):
    return jnp.bitwise_xor(index, bits)


def remote(src, dst, send, recv, dp, seq):
    return pltpu.make_async_remote_copy(
        src_ref=src,
        dst_ref=dst,
        send_sem=send,
        recv_sem=recv,
        device_id=(dp, seq),
        device_id_type=MESH,
    )


def greet(n_dp, n_seq):
    d, s = place()
    barrier = pltpu.get_barrier_semaphore()
    for off in range(1, n_dp):
        pl.semaphore_signal(
            barrier, inc=1, device_id=(xor(d, off), s), device_id_type=MESH
        )
    for off in range(1, n_seq):
        pl.semaphore_signal(
            barrier, inc=1, device_id=(d, lax.rem(s + off, n_seq)), device_id_type=MESH
        )
    pl.semaphore_wait(barrier, n_dp - 1 + n_seq - 1)


def bit_orders(n_dp):
    high = [1 << b for b in range(1, n_dp.bit_length() - 1)]
    return (high + [1], high[::-1] + [1])


def signed(value, sign):
    return value if sign > 0 else -value


class WeightGather:
    def __init__(self, shard, full, own_sem, z_send, z_recv, x_send, x_recv, n_dp, n_seq):
        self.shard, self.full, self.own_sem = shard, full, own_sem
        self.z_send, self.z_recv = z_send, z_recv
        self.x_send, self.x_recv = x_send, x_recv
        self.n_seq = n_seq
        self.cols = shard.shape[1] // 2
        self.orders = bit_orders(n_dp)
        self.steps = len(self.orders[0])
        self.groups = []
        for h in range(2):
            known = [(0, 0)]
            for step, bit in enumerate(self.orders[h]):
                known += [(off ^ bit, step + 1) for off, _ in known]
            self.groups.append(known)

    def own(self):
        d, s = place()
        return pltpu.make_async_copy(self.shard, self.full.at[d, s], self.own_sem)

    def z_copy(self, way, k):
        d, s = place()
        origin = s - signed(k - 1, way)
        side = 0 if way > 0 else 1
        src = self.shard if k == 1 else self.full.at[d, origin]
        return remote(
            src,
            self.full.at[d, origin],
            self.z_send.at[side, k],
            self.z_recv.at[side, k],
            d,
            s + way,
        )

    def direct_copy(self, way, k):
        d, s = place()
        side = 0 if way > 0 else 1
        return remote(
            self.shard,
            self.full.at[d, s],
            self.z_send.at[side, k],
            self.z_recv.at[side, k],
            d,
            s + signed(k, way),
        )

    def direct_each(self, body):
        d, s = place()
        for k in range(1, self.n_seq):
            for way in (1, -1):
                to = s + signed(k, way)

                @pl.when((to >= 0) & (to < self.n_seq))
                def _():
                    body(self.direct_copy(way, k))

    def z_valid(self, way, k):
        d, s = place()
        origin = s - signed(k - 1, way)
        to = s + way
        return (origin >= 0) & (origin < self.n_seq) & (to >= 0) & (to < self.n_seq)

    def x_copy(self, origin, h, off, bit, own=False):
        d, s = place()
        cols = pl.ds(h * self.cols, self.cols)
        dst = self.full.at[xor(d, off), origin, :, cols]
        src = self.shard.at[:, cols] if own else dst
        return remote(
            src,
            dst,
            self.x_send.at[origin, h, off ^ bit],
            self.x_recv.at[origin, h, off ^ bit],
            xor(d, bit),
            s,
        )

    def each(self, k, body):
        d, s = place()
        if k == 0:
            body(s, 0)
            return
        for way in (1, -1):
            origin = s - signed(k, way)

            @pl.when((origin >= 0) & (origin < self.n_seq))
            def _():
                body(origin, way)

    def z_start(self, k):
        for way in (1, -1):

            @pl.when(self.z_valid(way, k))
            def _():
                self.z_copy(way, k).start()

    def own_start(self):
        self.own().start()
        d, s = place()
        for h in range(2):
            for bit in self.orders[h]:
                self.x_copy(s, h, 0, bit, True).start()

    def event(self, k, t, forward=True):
        if t == 0:
            d, s = place()

            def arrival(origin, way):
                side = 0 if way > 0 else 1
                remote(
                    self.shard,
                    self.full.at[d, origin],
                    self.z_send.at[side, k],
                    self.z_recv.at[side, k],
                    d,
                    s,
                ).wait_recv()
                for h in range(2):
                    for bit in self.orders[h]:
                        self.x_copy(origin, h, 0, bit).start()

            self.each(k, arrival)
            if forward and k + 1 < self.n_seq:
                self.z_start(k + 1)
            return

        def passing(origin, way):
            for h in range(2):
                for off, step in self.groups[h]:
                    if step != t:
                        continue
                    self.x_copy(origin, h, off, 0).wait_recv()
                    for bit in self.orders[h][t:]:
                        self.x_copy(origin, h, off, bit).start()

        self.each(k, passing)

    def finish(self, direct=False):
        if direct:
            self.direct_each(lambda copy: copy.wait_send())
        for k in range(1, self.n_seq if not direct else 1):
            for way in (1, -1):

                @pl.when(self.z_valid(way, k))
                def _():
                    self.z_copy(way, k).wait_send()

        for k in range(self.n_seq):

            def sent(origin, way):
                for h in range(2):
                    for off, step in self.groups[h]:
                        for bit in self.orders[h][step:]:
                            self.x_copy(origin, h, off, bit).wait_send()

            self.each(k, sent)


def dot(a, b, dims):
    return lax.dot_general(a, b, (dims, ((), ())), preferred_element_type=F32)


def swap_halves(x):
    quarter = HEAD_DIM // 2
    lane = lax.broadcasted_iota(jnp.int32, x.shape, 1)
    return jnp.where(
        lax.rem(lane, HEAD_DIM) < quarter,
        pltpu.roll(x, 128 - quarter, axis=1),
        pltpu.roll(x, quarter, axis=1),
    )


def normalise(x):
    mean = jnp.mean(x, -1, keepdims=True)
    centred = x - mean
    var = jnp.mean(centred * centred, -1, keepdims=True)
    rstd = lax.rsqrt(var + EPSILON)
    return centred * rstd, rstd


def join_slabs(slabs, whole):
    depth = slabs.shape[-2]
    count = math.prod(slabs.shape[:-2])
    group = 16 // math.gcd(16, depth)

    @pl.loop(0, count // group)
    def _(i):
        parts = []
        for j in range(group):
            k, idx = i * group + j, []
            for n in slabs.shape[:-2][::-1]:
                idx.append(lax.rem(k, n))
                k = lax.div(k, n)
            parts.append(slabs[tuple(idx[::-1])])
        rows = group * depth
        whole[pl.ds(pl.multiple_of(i * rows, rows), rows), :] = jnp.concatenate(parts, 0)


def lanes_of(j, shape):
    lane = lax.broadcasted_iota(jnp.int32, shape, 1)
    return lax.div(lane, HEAD_DIM) == j


def front_kernel(n_dp, n_seq, rows, *refs):
    tokens, cot, seg, part, *shards = refs[:6]
    cos, sin = refs[6:8]
    tok_o, cot_o, doc_o, norm_o, pack_o, *fulls = refs[8:15]
    mod_o, mixed_o, lse_o = refs[15:18]
    (
        tok,
        segs,
        docs,
        normed,
        packed,
        w_in,
        w,
        values,
        keys,
        mod_in,
        mod_sum,
        mod_row,
        out_sem,
        row_send,
        row_recv,
        mod_send,
        mod_recv,
        modz_send,
        modz_recv,
        own_sem,
        z_send,
        z_recv,
        x_send,
        x_recv,
    ) = refs[18:]
    d, s = place()
    length, width = tokens.shape[1:]
    seq_len = length * n_seq
    first = lax.rem(d, 2)
    mine = s - first
    active = (mine >= 0) & (mine < rows)
    greet(n_dp, n_seq)

    def mod_copy(off):
        return remote(
            part.at[xor(d, off)],
            mod_in.at[d],
            mod_send.at[off],
            mod_recv.at[off],
            xor(d, off),
            s,
        )

    own_part = pltpu.make_async_copy(part.at[d], mod_in.at[d], mod_send.at[0])
    own_part.start()
    for off in range(1, n_dp):
        mod_copy(off).start()

    qkv, rest = [
        WeightGather(
            shards[i],
            fulls[i],
            own_sem.at[i],
            z_send.at[i],
            z_recv.at[i],
            x_send.at[i],
            x_recv.at[i],
            n_dp,
            n_seq,
        )
        for i in range(2)
    ]
    qkv.direct_each(lambda copy: copy.start())
    rest.z_start(1)
    qkv.own_start()

    trio = ((tokens, tok), (seg, segs), (cot, cot_o))

    def row_local(k, i):
        src, dst = trio[k]
        return pltpu.make_async_copy(src.at[i], dst.at[s], row_send.at[k, i])

    def row_remote(k, i):
        src, dst = trio[k]
        return remote(
            src.at[i], dst.at[s], row_send.at[k, i], row_recv.at[k, s], d, first + i
        )

    def row_start(k):
        for i in range(rows):

            @pl.when(first + i == s)
            def _():
                row_local(k, i).start()

            @pl.when(first + i != s)
            def _():
                row_remote(k, i).start()

    def row_sent(k):
        for i in range(rows):

            @pl.when(first + i != s)
            def _():
                row_remote(k, i).wait_send()

    def row_arrival(k, origin):
        src, dst = trio[k]
        remote(
            src.at[0],
            dst.at[origin],
            row_send.at[k, 0],
            row_recv.at[k, origin],
            d,
            origin,
        ).wait_recv()

    def row_own(k):
        for i in range(rows):

            @pl.when(first + i == s)
            def _():
                row_local(k, i).wait()

    def mod_exchange():
        own_part.wait()
        for off in range(1, n_dp):
            remote(
                part.at[d],
                mod_in.at[xor(d, off)],
                mod_send.at[off],
                mod_recv.at[off],
                d,
                s,
            ).wait_recv()
        total = mod_in[0]
        for e in range(1, n_dp):
            total += mod_in[e]
        mod_sum[...] = total
        for i in range(rows):

            @pl.when(first + i == s)
            def _():
                mod_row[s] = mod_sum[i]

            @pl.when(first + i != s)
            def _():
                remote(
                    mod_sum.at[i],
                    mod_row.at[s],
                    modz_send.at[i],
                    modz_recv.at[s],
                    d,
                    first + i,
                ).start()

    @pl.when(jnp.logical_not(active))
    def _():
        tok[...] = jnp.zeros_like(tok)
        segs[...] = jnp.zeros_like(segs)

    row_start(1)
    mod_exchange()
    row_start(0)
    for k in range(1, n_seq):
        qkv.event(k, 0, forward=False)
    for k in range(n_seq):
        qkv.event(k, 1)
    rest.own_start()
    rest.event(1, 0)
    for t in range(2, qkv.steps + 1):
        for k in range(n_seq):
            qkv.event(k, t)
    stage = pltpu.make_async_copy(fulls[0], w_in, out_sem.at[0])
    qkv.own().wait()
    stage.start()

    @pl.when(active)
    def _():
        for off in range(1, n_seq):
            row_arrival(1, lax.rem(s + off, n_seq))

    row_own(1)
    lane = lax.broadcasted_iota(jnp.int32, (length, 128), 1)
    lane = lax.rem(lane, HEAD_DIM).astype(F32)
    for z in range(n_seq):
        ids = jnp.transpose(
            jnp.broadcast_to(segs[z, 0:1, :].astype(F32), (128, length))
        )
        same = ids == lane
        at = pl.ds(z * length, length)
        docs[0, at, :] = jnp.where(
            same | ((lane >= 8.0) & (lane < 11.0)), 1.0, 0.0
        ).astype(BF16)
        docs[1, at, :] = jnp.where(same | (lane >= 8.0), 0.0, MASK_FILL).astype(BF16)
    doc_copy = pltpu.make_async_copy(docs, doc_o, out_sem.at[1])
    doc_copy.start()

    stage.wait()
    depth = w_in.shape[2]

    join_slabs(w_in, w)

    @pl.when(active)
    def _():
        for off in range(1, n_seq):
            origin = lax.rem(s + off, n_seq)
            remote(
                mod_sum.at[0],
                mod_row.at[origin],
                modz_send.at[0],
                modz_recv.at[origin],
                d,
                origin,
            ).wait_recv()
        total = mod_row[0]
        for z in range(1, n_seq):
            total += mod_row[z]
        mod_o[...] = total

    @pl.when(jnp.logical_not(active))
    def _():
        mod_o[...] = jnp.zeros_like(mod_o)

    rest.event(0, 1)

    gain = mod_o[6:7, :] * (1.0 + mod_o[1:2, :])
    shift = mod_o[0:1, :]
    row_own(0)
    for off in range(n_seq):
        z = lax.rem(s + off, n_seq)
        if off:

            @pl.when(active)
            def _():
                row_arrival(0, z)

        normal, _ = normalise(tok[z].astype(F32))
        at = pl.ds(pl.multiple_of(z * length, length), length)
        normed[at, :] = (normal * gain + shift).astype(BF16)
    outs = [
        pltpu.make_async_copy(tok, tok_o, out_sem.at[2]),
        pltpu.make_async_copy(normed, norm_o, out_sem.at[3]),
    ]
    for c in outs:
        c.start()

    for kind in range(3):

        @pl.loop(0, width // 256)
        def _(c):
            col = kind * width + c * 256
            wc = w[:, pl.ds(pl.multiple_of(col, 256), 256)]
            for r in range(seq_len // 256):
                at = pl.ds(r * 256, 256)
                y = dot(normed[at, :], wc, ((1,), (0,)))
                for j in range(2):
                    p = y[:, j * 128 : (j + 1) * 128]
                    if kind < 2:
                        p = p * cos[at, :] + swap_halves(p) * sin[at, :]
                    if kind == 0:
                        p = p * (LOG2E / math.sqrt(HEAD_DIM))
                    packed[kind * (width // 128) + c * 2 + j, at, :] = p.astype(BF16)

    pack_copy = pltpu.make_async_copy(packed, pack_o, out_sem.at[4])
    pack_copy.start()
    early = [(0, 2), (1, 1), (0, 3), (2, 0)]
    for e in early:
        rest.event(*e)
    row_start(2)
    pairs = width // 128
    slots = {
        1: [(1, 2)],
        2: [(3, 0), (2, 1), (1, 3)],
        4: [(2, 2)],
        5: [(3, 1)],
    }
    done = {e for v in slots.values() for e in v}
    done |= set(early) | {(1, 0), (0, 1)}

    values[:, 128:] = jnp.ones((seq_len, 128), BF16)
    block = 128
    lse_o[...] = jnp.zeros_like(lse_o)

    @pl.loop(0, pairs)
    def _(p):
        k = packed[pairs + p]
        values[:, :128] = packed[2 * pairs + p]
        for j in range(2):
            keys[j] = jnp.where(lanes_of(j, k.shape), k, docs[0])
        for i in range(seq_len // block):
            at = pl.ds(i * block, block)
            q = packed[p, at, :]
            both = []
            stats = lse_o[at, :]
            lane = lax.broadcasted_iota(jnp.int32, (block, 128), 1)
            for j in range(2):
                own = lanes_of(j, q.shape)
                scores = dot(jnp.where(own, q, docs[1, at, :]), keys[j], ((1,), (1,)))
                top = jnp.max(scores, -1, keepdims=True)
                e = jnp.exp2(scores - top).astype(BF16)
                o = dot(e, values[...], ((1,), (0,)))
                total = o[:, 128:]
                both.append(o[:, :128] / total)
                stats = jnp.where(lane == 2 * p + j, top + jnp.log2(total), stats)
            lse_o[at, :] = stats
            mixed_o[at, pl.ds(pl.multiple_of(p * 128, 128), 128)] = jnp.where(
                lane < HEAD_DIM, both[0], both[1]
            ).astype(BF16)
        for slot, events in slots.items():

            @pl.when(p == slot)
            def _():
                for k, t in events:
                    rest.event(k, t)

    for t in range(1, rest.steps + 1):
        for k in range(n_seq):
            if (k, t) not in done:
                rest.event(k, t)

    for i in range(rows):

        @pl.when(first + i != s)
        def _():
            remote(
                mod_sum.at[i], mod_row.at[s], modz_send.at[i], modz_recv.at[s], d, first + i
            ).wait_send()

    for off in range(1, n_dp):
        mod_copy(off).wait_send()
    rest.own().wait()
    for c in outs + [doc_copy, pack_copy]:
        c.wait()

    row_own(2)

    @pl.when(active)
    def _():
        for off in range(1, n_seq):
            row_arrival(2, lax.rem(s + off, n_seq))

    @pl.when(jnp.logical_not(active))
    def _():
        copies = [
            pltpu.make_async_copy(tok.at[z], cot_o.at[z], row_recv.at[2, z])
            for z in range(n_seq)
        ]
        for c in copies:
            c.start()
        for c in copies:
            c.wait()

    for k in range(3):
        row_sent(k)
    qkv.finish(direct=True)
    rest.finish()


def front(n_dp, n_seq, tokens, cot, seg, part, shards, cos, sin):
    rows, length, width = tokens.shape
    seq_len = length * n_seq
    dma = pltpu.SemaphoreType.DMA
    struct = jax.ShapeDtypeStruct
    pairs = width // 128
    outs = [
        struct((n_seq, length, width), BF16),
        struct((n_seq, length, width), BF16),
        struct((2, seq_len, 128), BF16),
        struct((seq_len, width), BF16),
        struct((3 * pairs, seq_len, 128), BF16),
    ]
    outs += [struct((n_dp, n_seq) + w.shape, BF16) for w in shards]
    outs += [
        struct((8, width), F32),
        struct((seq_len, width), BF16),
        struct((seq_len, 128), F32),
    ]
    return pl.pallas_call(
        functools.partial(front_kernel, n_dp, n_seq, rows),
        out_shape=outs,
        in_specs=[ANY] * 6 + [VMEM] * 2,
        out_specs=[ANY] * 7 + [VMEM] * 3,
        scratch_shapes=[
            pltpu.VMEM((n_seq, length, width), BF16),
            pltpu.VMEM((n_seq,) + seg.shape[1:], jnp.int32),
            pltpu.VMEM((2, seq_len, 128), BF16),
            pltpu.VMEM((seq_len, width), BF16),
            pltpu.VMEM((3 * pairs, seq_len, 128), BF16),
            pltpu.VMEM((n_dp, n_seq) + shards[0].shape, BF16),
            pltpu.VMEM((width, 3 * width), BF16),
            pltpu.VMEM((seq_len, 256), BF16),
            pltpu.VMEM((2, seq_len, 128), BF16),
            pltpu.VMEM((n_dp, rows, 8, width), F32),
            pltpu.VMEM((rows, 8, width), F32),
            pltpu.VMEM((n_seq, 8, width), F32),
            dma((5,)),
            dma((3, rows)),
            dma((3, n_seq)),
            dma((n_dp,)),
            dma((n_dp,)),
            dma((rows,)),
            dma((n_seq,)),
            dma((2,)),
            dma((2, 2, n_seq)),
            dma((2, 2, n_seq)),
            dma((2, n_seq, 2, n_dp)),
            dma((2, n_seq, 2, n_dp)),
        ],
        compiler_params=pltpu.CompilerParams(
            collective_id=0, has_side_effects=True, vmem_limit_bytes=VMEM_LIMIT
        ),
    )(tokens, cot, seg, part, *shards, cos, sin)


def split3(x):
    high = x.astype(BF16)
    x = x - high.astype(F32)
    middle = x.astype(BF16)
    low = (x - middle.astype(F32)).astype(BF16)
    return high, middle, low


class GradReduce:
    def __init__(self, grad, own, local, core_in, step_in, z_in, sems, n_dp, n_seq):
        self.grad, self.own, self.local = grad, own, local
        self.core_in, self.step_in, self.z_in = core_in, step_in, z_in
        self.sems, self.n_seq = sems, n_seq
        self.bits = list(range(n_dp.bit_length() - 2, 0, -1))
        self.m = len(self.bits)
        self.orders = (list(range(self.m)), list(range(self.m))[::-1])
        self.cols = core_in.shape[-1] // 2

    def my(self, dim):
        d, _ = place()
        return lax.rem(lax.div(d, 1 << self.bits[dim]), 2)

    def mine(self):
        return tuple(self.my(dim) for dim in range(self.m))

    def index(self, done, flip=None):
        return tuple(
            self.my(dim)
            if dim in done
            else 1 - self.my(dim)
            if dim == flip
            else slice(None)
            for dim in range(self.m)
        )

    def core_copies(self, z):
        d, s = place()
        core = lax.rem(d, 2)
        lead = (slice(None),) * self.m
        send, recv, local = self.sems["core"]
        copies = [
            remote(
                self.grad.at[lead + (1 - core, z)],
                self.core_in.at[lead + (z,)],
                send.at[z],
                recv.at[z],
                xor(d, 1),
                s,
            )
        ]
        if self.local:
            copies.append(
                pltpu.make_async_copy(
                    self.grad.at[lead + (core, z)],
                    self.own(lead, z, slice(None)),
                    local.at[z],
                )
            )
        return copies

    def core_start(self, z):
        for c in self.core_copies(z):
            c.start()

    def core_add(self, z):
        for c in self.core_copies(z):
            c.wait()

        @pl.loop(0, 1 << self.m)
        def _(n):
            lead = tuple(
                lax.rem(lax.div(n, 1 << (self.m - 1 - dim)), 2) for dim in range(self.m)
            )
            target = self.own(lead, z, slice(None))
            target[...] = target[...] + self.core_in[lead + (z,)]

    def step_copy(self, z, h, step):
        d, s = place()
        order = self.orders[h]
        send, recv = self.sems["step"]
        cols = pl.ds(h * self.cols, self.cols)
        return remote(
            self.own(self.index(order[:step], order[step]), z, cols),
            self.step_in[h][step].at[z],
            send.at[z, h, step],
            recv.at[z, h, step],
            xor(d, 1 << self.bits[order[step]]),
            s,
        )

    def z_copy(self, z):
        d, s = place()
        send, recv = self.sems["z"]
        return remote(
            self.own(self.mine(), z, slice(None)),
            self.z_in.at[s],
            send.at[z],
            recv.at[s],
            d,
            z,
        )

    def event(self, z, t):
        for h in range(2):
            if t:
                self.step_copy(z, h, t - 1).wait()
                order = self.orders[h]
                cols = pl.ds(h * self.cols, self.cols)
                free = [dim for dim in range(self.m) if dim not in order[:t]]
                for n in range(1 << len(free)):
                    bits = [(n >> (len(free) - 1 - i)) & 1 for i in range(len(free))]
                    lead = tuple(
                        bits[free.index(dim)] if dim in free else self.my(dim)
                        for dim in range(self.m)
                    )
                    target = self.own(lead, z, cols)
                    target[...] = target[...] + self.step_in[h][t - 1][(z, *bits)]
            if t < self.m:
                self.step_copy(z, h, t).start()
        if t == self.m:
            _, s = place()

            @pl.when(z != s)
            def _():
                self.z_copy(z).start()

    def total(self):
        d, s = place()
        send, recv = self.sems["z"]
        for off in range(1, self.n_seq):
            origin = lax.rem(s + off, self.n_seq)
            remote(
                self.own(self.mine(), s, slice(None)),
                self.z_in.at[origin],
                send.at[origin],
                recv.at[origin],
                d,
                origin,
            ).wait_recv()
        total = self.own(self.mine(), s, slice(None))[...].astype(F32)
        for off in range(1, self.n_seq):
            total += self.z_in[lax.rem(s + off, self.n_seq)].astype(F32)
        return total

    def sent(self):
        _, s = place()
        for z in range(self.n_seq):

            @pl.when(z != s)
            def _():
                self.z_copy(z).wait_send()


def back_kernel(n_dp, n_seq, rows, hidden, *refs):
    grad_rest, out_row, wq_full, packed_h, mixed_h, grad_mixed_h, normed_h = refs[:7]
    lse, docs, cos, sin, tok, grad_mid, mod, gm_in = refs[7:15]
    gq_o, go_o, gu_o, gd_o = refs[15:19]
    out_o, dtok_o, gmod_o = refs[19:22]
    refs = refs[22:]
    m = n_dp.bit_length() - 2
    acc_r, core_r, zin_r = refs[:3]
    step_r = (refs[3 : 3 + m], refs[3 + m : 3 + 2 * m])
    refs = refs[3 + 2 * m :]
    w_in, core_q, zin_q = refs[:3]
    step_q = (refs[3 : 3 + m], refs[3 + m : 3 + 2 * m])
    refs = refs[3 + 2 * m :]
    (
        w,
        qkv,
        normed_t,
        grad_qkv,
        dtok,
        q2,
        k2,
        v2,
        g2,
        dq2,
        gmod,
        qkv_sem,
        w_sem,
        row_send,
        row_recv,
        g_send,
        g_recv,
        gd_send,
        gd_recv,
        c_send,
        c_recv,
        c_local,
        s_send,
        s_recv,
        z_send,
        z_recv,
    ) = refs
    d, s = place()
    length, width = out_row.shape[1:]
    seq_len = length * n_seq
    pairs = width // 128
    first = lax.rem(d, 2)
    mine = s - first
    active = (mine >= 0) & (mine < rows)
    core = lax.rem(d, 2)

    def pair_copies(p, slot):
        return [
            pltpu.make_async_copy(
                packed_h.at[kind * pairs + p], qkv.at[slot, kind], qkv_sem.at[slot, kind]
            )
            for kind in range(3)
        ] + [
            pltpu.make_async_copy(
                src.at[:, pl.ds(pl.multiple_of(p * 128, 128), 128)],
                qkv.at[slot, kind],
                qkv_sem.at[slot, kind],
            )
            for kind, src in ((3, mixed_h), (4, grad_mixed_h))
        ]

    for c in pair_copies(0, 0):
        c.start()
    w_copy = pltpu.make_async_copy(wq_full, w_in, w_sem.at[0])
    w_copy.start()
    normed_copy = pltpu.make_async_copy(normed_h, dtok, w_sem.at[1])
    normed_copy.start()
    greet(n_dp, n_seq)

    def sems(i):
        return {
            "core": (c_send.at[i], c_recv.at[i], c_local.at[i]),
            "step": (s_send.at[i], s_recv.at[i]),
            "z": (z_send.at[i], z_recv.at[i]),
        }

    rest = GradReduce(
        grad_rest,
        lambda lead, z, cols: acc_r.at[tuple(lead) + (z, slice(None), cols)],
        True,
        core_r,
        step_r,
        zin_r,
        sems(0),
        n_dp,
        n_seq,
    )
    stage = w_in
    last = GradReduce(
        stage,
        lambda lead, z, cols: stage.at[tuple(lead) + (core, z, slice(None), cols)],
        False,
        core_q,
        step_q,
        zin_q,
        sems(1),
        n_dp,
        n_seq,
    )
    for z in range(n_seq):
        rest.core_start(z)

    pair = ((out_row, out_o), (dtok, dtok_o))

    def row_local(k):
        src, dst = pair[k]
        return pltpu.make_async_copy(src.at[s], dst.at[mine], row_send.at[k, 0])

    def row_remote(k, off):
        src, dst = pair[k]
        to = lax.rem(s + off, n_seq)
        return remote(
            src.at[to], dst.at[mine], row_send.at[k, off], row_recv.at[k, mine], d, to
        )

    def row_start(k):
        @pl.when(active)
        def _():
            row_local(k).start()
            for off in range(1, n_seq):
                row_remote(k, off).start()

    def row_sent(k):
        @pl.when(active)
        def _():
            row_local(k).wait()
            for off in range(1, n_seq):
                row_remote(k, off).wait_send()

    def row_arrivals(k):
        src, dst = pair[k]
        for i in range(rows):

            @pl.when(first + i != s)
            def _():
                remote(
                    src.at[0],
                    dst.at[i],
                    row_send.at[k, 0],
                    row_recv.at[k, i],
                    d,
                    first + i,
                ).wait_recv()

    row_start(0)

    w_copy.wait()
    depth = w_in.shape[-2]
    lead_dims = w_in.shape[:-2]

    join_slabs(w_in, w)
    normed_copy.wait()
    for r in range(n_seq):
        normed_t[:, pl.ds(r * length, length)] = jnp.transpose(dtok[r])

    rest.core_add(0)
    rest.event(0, 0)
    rest.core_add(1)
    rest.event(1, 0)
    slots = {
        0: [("c", 2), ("c", 3)],
        2: [(0, 1)],
        3: [(2, 0)],
        4: [(1, 1)],
        5: [(0, 2), (3, 0)],
        7: [(2, 1)],
        8: [(1, 2)],
        10: [(3, 1)],
        11: [(2, 2)],
    }
    done = {e for v in slots.values() for e in v} | {(0, 0), (1, 0)}
    block = seq_len // 2
    lane = lax.broadcasted_iota(jnp.int32, (seq_len, 128), 1)

    @pl.loop(0, pairs)
    def _(p):
        now = lax.rem(p, 2)

        @pl.when(p + 1 < pairs)
        def _():
            for c in pair_copies(p + 1, 1 - now):
                c.start()

        for c in pair_copies(p, now):
            c.wait()
        queries, keys, values = qkv[now, 0], qkv[now, 1], qkv[now, 2]
        at_p = pl.ds(pl.multiple_of(p * 128, 128), 128)
        grads = qkv[now, 4]
        product = grads.astype(F32) * qkv[now, 3].astype(F32)
        nothing = jnp.zeros_like(grads)
        for j in range(2):
            own = lanes_of(j, grads.shape)
            base = HEAD_DIM * (1 - j) + 8

            def with_terms(x, other, column):
                for n, term in enumerate(split3(column)):
                    other = jnp.where(lane == base + n, term, other)
                return jnp.where(own, x, other)

            inner = jnp.sum(jnp.where(own, product, 0.0), -1, keepdims=True)
            stat = jnp.sum(jnp.where(lane == 2 * p + j, lse[...], 0.0), -1, keepdims=True)
            g2[j] = with_terms(grads, nothing, -inner)
            q2[j] = with_terms(queries, docs[1], -stat)
            k2[j] = jnp.where(own, keys, docs[0])
            v2[j] = jnp.where(own, values, docs[0])
        for i in range(seq_len // block):
            at = pl.ds(i * block, block)
            dvs, dks = [], []
            for j in range(2):
                probs = jnp.exp2(dot(k2[j, at, :], q2[j], ((1,), (1,))))
                ds = probs * dot(v2[j, at, :], g2[j], ((1,), (1,)))
                ds = ds.astype(BF16)
                dvs.append(dot(probs.astype(BF16), grads, ((1,), (0,))))
                dks.append(dot(ds, queries, ((1,), (0,))))
                dq = dot(ds, qkv[now, 1, at, :], ((0,), (0,)))
                if i == 0:
                    dq2[j] = dq
                else:
                    dq2[j] += dq
            here = lanes_of(0, dvs[0].shape)
            dk = jnp.where(here, dks[0], dks[1]) * (1.0 / LOG2E)
            grad_qkv[at, pl.ds(pl.multiple_of(width + p * 128, 128), 128)] = (
                dk * cos[at, :] + swap_halves(dk * sin[at, :])
            ).astype(BF16)
            grad_qkv[at, pl.ds(pl.multiple_of(2 * width + p * 128, 128), 128)] = jnp.where(
                here, dvs[0], dvs[1]
            ).astype(BF16)
            for slot, events in slots.items():
                if slot % 2 != i:
                    continue

                @pl.when(p == slot // 2)
                def _():
                    for z, t in events:
                        if z == "c":
                            rest.core_add(t)
                        else:
                            rest.event(z, t)

        dq = jnp.where(lanes_of(0, dq2.shape[1:]), dq2[0], dq2[1])
        dq = dq * (1.0 / math.sqrt(HEAD_DIM))
        grad_qkv[:, at_p] = (dq * cos[...] + swap_halves(dq * sin[...])).astype(BF16)

    gain = mod[6:7, :]
    scale = 1.0 + mod[1:2, :]
    gmod[...] = gm_in[...]
    for r in range(n_seq):
        at = pl.ds(r * length, length)
        e = dot(grad_qkv[at, :], w[...], ((1,), (1,)))
        normal, rstd = normalise(tok[at, :].astype(F32))
        gmod[0:1, :] += jnp.sum(e, 0, keepdims=True)
        weighted = jnp.sum(e * normal, 0, keepdims=True)
        gmod[1:2, :] += weighted * gain
        gmod[6:7, :] += weighted * scale
        h = e * (gain * scale)
        mean_h = jnp.mean(h, -1, keepdims=True)
        mean_hz = jnp.mean(h * normal, -1, keepdims=True)
        dtok[r] = (grad_mid[at, :] + (h - mean_h - normal * mean_hz) * rstd).astype(BF16)

    own_row = pltpu.make_async_copy(gmod, gmod_o.at[d, mine], g_send.at[0])

    def group_copy(off):
        return remote(
            gmod,
            gmod_o.at[d, mine],
            g_send.at[off],
            g_recv.at[s],
            d,
            lax.rem(s + off, n_seq),
        )

    @pl.when(active)
    def _():
        own_row.start()
        for off in range(1, n_seq):
            group_copy(off).start()

    row_start(1)

    for c in range(3 * width // 256):
        cols = pl.ds(c * 256, 256)
        g = dot(normed_t[...], grad_qkv[:, cols], ((1,), (0,)))
        for i in range(n_dp * n_seq):
            k, idx = i, []
            for n in lead_dims[::-1]:
                idx.append(k % n)
                k //= n
            stage[tuple(idx[::-1]) + (slice(None), cols)] = g[
                i * depth : (i + 1) * depth
            ].astype(BF16)
    for z in range(n_seq):
        last.core_start(z)
    for z in range(n_seq):
        for t in range(m + 1):
            if (z, t) not in done:
                rest.event(z, t)
    for z in range(n_seq):
        last.core_add(z)
        last.event(z, 0)

    @pl.when(active)
    def _():
        own_row.wait()

    for i in range(rows):
        owner = first + i

        @pl.when(owner != s)
        def _():
            remote(
                gmod, gmod_o.at[d, i], g_send.at[0], g_recv.at[owner], d, owner
            ).wait_recv()

    def dp_copy(off):
        return remote(
            gmod_o.at[d], gmod_o.at[d], gd_send.at[off], gd_recv.at[off], xor(d, off), s
        )

    for off in range(1, n_dp):
        dp_copy(off).start()
    for t in range(1, m + 1):
        for z in range(n_seq):
            last.event(z, t)
    total = rest.total()
    go_o[...] = total[:, :width]
    gu_o[...] = total[:, width : width + hidden]
    for i in range(hidden // width):
        col = width + hidden + i * width
        gd_o[i * depth : (i + 1) * depth, :] = total[:, col : col + width]
    gq_o[...] = last.total()

    for off in range(1, n_dp):
        e = xor(d, off)
        dp_copy(off).wait_send()
        remote(
            gmod_o.at[e], gmod_o.at[e], gd_send.at[off], gd_recv.at[off], e, s
        ).wait_recv()

    @pl.when(active)
    def _():
        for off in range(1, n_seq):
            group_copy(off).wait_send()

    for k in range(2):
        row_sent(k)
        row_arrivals(k)
    rest.sent()
    last.sent()


def back(n_dp, n_seq, rows, hidden, grad_rest, out_row, wq, hbm_args, vmem_args):
    dma = pltpu.SemaphoreType.DMA
    struct = jax.ShapeDtypeStruct
    m = n_dp.bit_length() - 2
    lead = (2,) * m
    length, width = out_row.shape[1:]
    seq_len = length * n_seq
    depth = wq.shape[-2]
    wide = grad_rest.shape[-1]
    gmod = vmem_args[-1]
    outs = [
        struct((depth, 3 * width), F32),
        struct((depth, width), F32),
        struct((depth, hidden), F32),
        struct((depth * hidden // width, width), F32),
        struct((rows, length, width), BF16),
        struct((rows, length, width), BF16),
        struct((n_dp, rows) + gmod.shape, F32),
    ]

    def reduce_scratch(n, acc):
        slabs = [
            pltpu.VMEM(acc + (n_seq, depth, n), BF16),
            pltpu.VMEM(lead + (n_seq, depth, n), BF16),
            pltpu.VMEM((n_seq, depth, n), BF16),
        ]
        for _ in range(2):
            for step in range(m):
                slabs.append(
                    pltpu.VMEM(
                        (n_seq,) + (2,) * (m - 1 - step) + (depth, n // 2), BF16
                    )
                )
        return slabs

    scratch = (
        reduce_scratch(wide, lead)
        + reduce_scratch(3 * width, lead + (2,))
        + [
            pltpu.VMEM((width, 3 * width), BF16),
            pltpu.VMEM((2, 5, seq_len, 128), BF16),
            pltpu.VMEM((width, seq_len), BF16),
            pltpu.VMEM((seq_len, 3 * width), BF16),
            pltpu.VMEM((n_seq, length, width), BF16),
        ]
        + [pltpu.VMEM((2, seq_len, 128), BF16)] * 4
        + [
            pltpu.VMEM((2, seq_len, 128), F32),
            pltpu.VMEM(gmod.shape, F32),
            dma((2, 5)),
            dma((2,)),
            dma((2, n_seq)),
            dma((2, rows)),
            dma((n_seq,)),
            dma((n_seq,)),
            dma((n_dp,)),
            dma((n_dp,)),
            dma((2, n_seq)),
            dma((2, n_seq)),
            dma((2, n_seq)),
            dma((2, n_seq, 2, m)),
            dma((2, n_seq, 2, m)),
            dma((2, n_seq)),
            dma((2, n_seq)),
        ]
    )
    split = lead + (2, n_seq)
    return pl.pallas_call(
        functools.partial(back_kernel, n_dp, n_seq, rows, hidden),
        out_shape=outs,
        in_specs=[ANY] * 7 + [VMEM] * len(vmem_args),
        out_specs=[VMEM] * 4 + [ANY] * 3,
        scratch_shapes=scratch,
        compiler_params=pltpu.CompilerParams(
            collective_id=1, has_side_effects=True, vmem_limit_bytes=VMEM_LIMIT
        ),
    )(
        grad_rest.reshape(split + grad_rest.shape[-2:]),
        out_row,
        wq.reshape(split + wq.shape[-2:]),
        *hbm_args,
        *vmem_args,
    )


def rotary_tables(seq_len):
    half = HEAD_DIM // 2
    freq = np.exp(np.float32(-math.log(10000.0)) * np.arange(half, dtype=np.float32) / np.float32(half))
    angles = np.arange(seq_len, dtype=np.float32)[:, None] * freq.astype(np.float32)[None, :]
    cos = np.tile(np.cos(angles), (1, 4)).astype(np.float32)
    sin = np.sin(angles)
    sin = np.concatenate([-sin, sin, -sin, sin], 1).astype(np.float32)
    return jnp.asarray(cos), jnp.asarray(sin)


def time_embed(step_ids, model_dim):
    half_dim = model_dim // 2
    frequency = jnp.exp(-math.log(10000.0) * jnp.arange(half_dim, dtype=jnp.float32) / half_dim)
    angles = step_ids.astype(jnp.float32)[:, None] * frequency[None, :]
    return jnp.concatenate([jnp.cos(angles), jnp.sin(angles)], axis=-1)


def modulate(inputs, norm_gain, mod_scale, mod_shift):
    average = jnp.mean(inputs, -1, keepdims=True)
    centred = inputs - average
    variance = jnp.mean(centred * centred, -1, keepdims=True)
    return centred * lax.rsqrt(variance + EPSILON) * norm_gain * (1.0 + mod_scale) + mod_shift


def matmul(a, b, spec):
    return jnp.einsum(spec, a, b, preferred_element_type=F32)


def placed_at(vector, index, length):
    whole = jnp.zeros((length,), F32)
    return lax.dynamic_update_slice(whole, vector.astype(F32), (index * vector.shape[0],))


def shards(
    n_dp,
    n_seq,
    tokens,
    segments,
    timesteps,
    w_mod,
    b_mod,
    gain_attn,
    w_qkv,
    w_out,
    gain_mlp,
    w_up,
    w_down,
    cotangent,
):
    rows, length, width = tokens.shape
    seq_len = length * n_seq
    hidden = w_up.shape[1]
    d, s = place()
    me = d * n_seq + s
    depth = w_mod.shape[0]
    cos, sin = rotary_tables(seq_len)

    steps = lax.all_gather(timesteps, "dp", axis=0, tiled=True)
    embedding = lax.dynamic_slice_in_dim(
        time_embed(steps, width).astype(BF16), me * depth, depth, 1
    )
    part = matmul(embedding, w_mod, "rk,kn->rn") + placed_at(b_mod, me, 6 * width)
    gains = jnp.concatenate(
        [placed_at(gain_attn, me, width), placed_at(gain_mlp, me, width)]
    )
    part = jnp.concatenate([part, jnp.broadcast_to(gains, (part.shape[0], 2 * width))], 1)
    part = part.reshape(n_dp, rows, 8, width)
    seg = jnp.broadcast_to(segments[:, None, :], (rows, 8, length))

    packed_rest = jnp.concatenate(
        [w_out, w_up]
        + [w_down[i * depth : (i + 1) * depth] for i in range(hidden // width)],
        1,
    )
    tok, cot, docs, normed_a, packed, wq, rest, mod, mixed, lse = front(
        n_dp, n_seq, tokens, cotangent, seg, part, (w_qkv, packed_rest), cos, sin
    )
    tok = tok.reshape(seq_len, width)
    cot = cot.reshape(seq_len, width).astype(F32)
    wo = rest[..., :width].reshape(width, width)
    wu = rest[..., width : width + hidden].reshape(width, hidden)
    wd = jnp.stack(
        [
            rest[..., width + hidden + i * width : width + hidden + (i + 1) * width]
            for i in range(hidden // width)
        ],
        2,
    ).reshape(hidden, width)
    shift_a, scale_a, gate_a, shift_m, scale_m, gate_m, gain_a, gain_m = (
        mod[j : j + 1] for j in range(8)
    )

    stream = tok.astype(F32)
    attn_out = matmul(mixed, wo, "td,de->te")
    middle = stream + gate_a * attn_out
    normed_m, norm_back_m = jax.vjp(modulate, middle, gain_m, scale_m, shift_m)
    normed_m = normed_m.astype(BF16)
    up_proj = matmul(normed_m, wu, "td,df->tf")
    activated, gelu_back = jax.vjp(jax.nn.gelu, up_proj)
    activated = activated.astype(BF16)
    mlp_out = matmul(activated, wd, "tf,fd->td")
    output = (middle + gate_m * mlp_out).astype(BF16)

    grad_mlp = (cot * gate_m).astype(BF16)
    grad_gate_m = jnp.sum(cot * mlp_out, 0, keepdims=True)
    grad_down = matmul(activated, grad_mlp, "tf,td->fd").astype(BF16)
    grad_act = matmul(grad_mlp, wd, "td,fd->tf")
    grad_up = gelu_back(grad_act)[0].astype(BF16)
    grad_wup = matmul(normed_m, grad_up, "td,tf->df").astype(BF16)
    grad_hm = matmul(grad_up, wu, "tf,df->td")
    grad_mid_norm, grad_gain_m, grad_scale_m, grad_shift_m = norm_back_m(grad_hm)
    grad_mid = cot + grad_mid_norm
    grad_gate_a = jnp.sum(grad_mid * attn_out, 0, keepdims=True)
    grad_attn = (grad_mid * gate_a).astype(BF16)
    grad_wout = matmul(mixed, grad_attn, "td,te->de").astype(BF16)
    grad_mixed = matmul(grad_attn, wo, "te,de->td").astype(BF16)

    gm_in = jnp.concatenate(
        [
            jnp.zeros((2, width), F32),
            grad_gate_a,
            grad_shift_m,
            grad_scale_m,
            grad_gate_m,
            jnp.zeros((1, width), F32),
            grad_gain_m,
        ],
        0,
    )

    def cut(g, n):
        return g.reshape((n_dp, n_seq, n * depth, -1))

    down = cut(grad_down, hidden // width)
    grad_rest = jnp.concatenate(
        [cut(grad_wout, 1), cut(grad_wup, 1)]
        + [down[:, :, i * depth : (i + 1) * depth] for i in range(hidden // width)],
        -1,
    )
    g_wqkv, g_wout, g_wup, g_wdown, out, d_tok, gmods = back(
        n_dp,
        n_seq,
        rows,
        hidden,
        grad_rest,
        output.reshape(n_seq, length, width),
        wq,
        (packed, mixed, grad_mixed, normed_a.reshape(n_seq, length, width)),
        (
            lse,
            docs,
            cos,
            sin,
            tok,
            grad_mid.astype(BF16),
            mod,
            gm_in,
        ),
    )
    gmods = gmods.reshape(n_dp * rows, 8 * width)
    g_w_mod = jnp.dot(
        embedding.astype(F32).T,
        gmods[:, : 6 * width],
        precision=lax.Precision.HIGHEST,
        preferred_element_type=F32,
    )
    summed = jnp.sum(gmods, 0)

    def own_part(vector, n):
        return lax.dynamic_slice_in_dim(vector, me * n, n, 0)

    return (
        out,
        d_tok,
        g_w_mod,
        own_part(summed[: 6 * width], b_mod.shape[0]),
        own_part(summed[6 * width : 7 * width], gain_attn.shape[0]),
        g_wqkv,
        g_wout,
        own_part(summed[7 * width :], gain_mlp.shape[0]),
        g_wup,
        g_wdown,
    )


def solution(mesh):
    both = P(("dp", "seq"))
    wide = P(("dp", "seq"), None)
    tokens = P("dp", "seq", None)
    return jax.shard_map(
        functools.partial(shards, mesh.shape["dp"], mesh.shape["seq"]),
        mesh=mesh,
        in_specs=(
            tokens,
            P("dp", "seq"),
            P("dp"),
            wide,
            both,
            both,
            wide,
            wide,
            both,
            wide,
            wide,
            tokens,
        ),
        out_specs=(tokens, tokens, wide, both, both, wide, wide, both, wide, wide),
        check_vma=False,
    )
```

time: 442 us -> 356 us (0.81)
  Pallas kernels: 307 us -> 221 us
  local copies, waits for them, and re-layouts: 17.9 us -> 35.3 us
  matrix products: 87.5 us -> 73.5 us
  other arithmetic: 15.7 us -> 10.9 us
    pallas_call x5 -> x2, Pallas kernels: 307 us -> 221 us  [the longest x1 126 us: back(): pl.pallas_call(functools.partial(back_kernel, n_dp, n_seq, rows, hidden),...]
    dot_general x12 -> x10, matrix products: 86.3 us -> 72.2 us  [matmul(): return jnp.einsum(spec, a, b, preferred_element_type=F32)]
    unnamed x65 -> x71, local copies, waits for them, and re-layouts: 12.7 us -> 23 us
    slice x1 -> x2, local copies, waits for them, and re-layouts: 0.88 us -> 5.9 us  [the longest x1 3.41 us: shards(): wu = rest[..., width:width + hidden].reshape(width, hidden)]
where the time goes in v2:
time: 356 us; the launch traced here: 350 us
  Pallas kernels  221 us (62%)
  matrix products  73.5 us (21%)
  local copies, waits for them, and re-layouts  35.3 us (10%)
  other arithmetic  10.9 us (3%)
  blocking collectives  8.01 us (2%)
    pallas_call x1, Pallas kernels, back(): pl.pallas_call(functools.partial(back_kernel, n_dp, n_seq, rows, hidden),...  126 us
    pallas_call x1, Pallas kernels, front(): pl.pallas_call(functools.partial(front_kernel, n_dp, n_seq, rows), out_sh...  95.1 us
    dot_general x10, matrix products, matmul(): return jnp.einsum(spec, a, b, preferred_element_type=F32)  72.2 us
    unnamed x71, local copies, waits for them, and re-layouts  23 us
    unnamed x1, blocking collectives  8.01 us

profile of v2, /device:TPU:24, one launch (start us, length us, event | category | flops | bytes accessed | tf_op | source)
XLA Modules:
  0.0 350.4 jit_solution(10047321847707211111)
XLA Ops:
  0.6 0.0 copy-start
  0.7 1.3 dynamic-slice.2
  2.6 0.9 dynamic-update-slice
  3.5 8.0 %all-reduce = s32[24]{0:T(128)S(1)} all-reduce(s32[24]{0:T(128)S(1)} %dynamic-update-slice), channel_id=1, replica_groups=mesh['dp'=8,'seq'=4] {'dp'}, use_global_device_ids=true, to_apply=%add | all-reduce | flops 24 | bytes 192
  11.5 0.8 convert_dynamic-update-slice_fusion.1
  12.3 0.7 convert_dynamic-update-slice_fusion.2
  13.0 0.8 convert_dynamic-update-slice_fusion
  13.8 1.3 broadcast_in_dim.16.refs_2_
  15.1 0.2 fusion.13
  15.3 0.8 constant_dynamic-update-slice_fusion.1
  16.1 0.9 constant_dynamic-update-slice_fusion
  17.0 0.8 slice_dynamic-update-slice_fusion.3
  17.8 0.8 slice_dynamic-update-slice_fusion.2
  18.6 0.8 slice_dynamic-update-slice_fusion.1
  19.3 0.8 slice_dynamic-update-slice_fusion.refs_5_
  20.1 0.0 copy-done
  20.1 0.3 convolution_add_fusion
  20.4 0.1 pad_maximum_fusion.1
  20.5 1.0 copy.25
  21.5 0.0 copy-done.16
  21.5 95.1 %shard_map.213 = (bf16[4,256,768]{2,1,0:T(8,128)(2,1)}, bf16[4,256,768]{2,1,0:T(8,128)(2,1)}, bf16[2,1024,128]{2,1,0:T(8,128)(2,1)}, bf16[1024,768]{1,0:T(8,128)...) custom-call(bf16[3,256,768]{2,1,0:T(8,128)(2,1)} %refs_0_.1, ...), custom_call_target="tpu_custom_call" | custom-call | tf_op jit(solution)/shard_map/pallas_call | solution.py:642
  116.5 1.0 slice_reduce_fusion.3
  117.5 3.0 fusion.7
  120.5 3.4 slice.88
  123.9 0.1 copy-done.2
  124.0 0.7 slice_bitcast_fusion.3
  124.7 0.6 pad_maximum_fusion
  125.4 0.6 copy.24
  126.0 0.8 copy-done.3
  126.7 0.5 copy-done.4
  127.2 1.6 fusion.23
  128.9 0.5 multiply_reduce_fusion.4
  129.4 8.4 %fusion.20 = f32[1024,3072]{1,0:T(8,128)} fusion(bf16[768,3072]{1,0:T(8,128)(2,1)S(1)} %bitcast.71, f32[1024,768]{1,0:T(8,128)S(1)} %get-tuple-element.58, f32[768]{0:T(1024)S(1)} %get-tuple-element.49, f32[768]{0:T(1024)S(1)} %get-tuple-element.50, f32[768]{0:T(1024)S(1)} %get-tuple-element.51, f32[1024]{0:T(1024)S(1)} %fusion.15, ...), kind=kOutput, calls=%fused_computation.78 | convolution fusion | flops 4836556800 | bytes 20464640 | tf_op jit(solution)/shard_map/td,df->tf/dot_general | solution.py:1296
  137.8 15.4 %fusion.6 = bf16[1024,3072]{1,0:T(8,128)(2,1)} fusion(f32[1024,3072]{1,0:T(8,128)} %fusion.20, bf16[1024,768]{1,0:T(8,128)(2,1)S(1)} %bitcast.81, bf16[3072,768]{1,0:T(8,128)(2,1)S(1)} %bitcast.69), kind=kOutput, calls=%fused_computation.8 | convolution fusion | flops 4894752768 | bytes 25165824 | tf_op jit(solution)/shard_map/td,fd->tf/dot_general | solution.py:1296
  153.2 10.0 %multiply_reduce_fusion = (f32[768]{0:T(1024)S(1)}, f32[1024]{0:T(1024)S(1)}, f32[768]{0:T(1024)S(1)}, f32[768]{0:T(1024)S(1)}, f32[1024,768]{1,0:T(8,128)}) fusion(f32[1024,768]{1,0:T(8,128)S(1)} %get-tuple-element.58, f32[768]{0:T(1024)S(1)} %get-tuple-element.50, f32[1024]{0:T(1024)S(1)} %fusion.15, f32[1024]{0:T(1024)S(1)} %broadcast_multiply_fusion, ...), kind=kOutput, calls=%fused_computation.22 | convolution fusion | flops 4841271296 | bytes 17329152 | tf_op jit(solution)/shard_map/tf,df->td/dot_general | solution.py:1296
  163.3 7.7 %convolution_convert_fusion.1 = bf16[768,3072]{1,0:T(8,128)(2,1)} fusion(bf16[1024,3072]{1,0:T(8,128)(2,1)S(1)} %copy-done.21, f32[1024,768]{1,0:T(8,128)S(1)} %get-tuple-element.58, f32[768]{0:T(1024)S(1)} %get-tuple-element.49, f32[768]{0:T(1024)S(1)} %get-tuple-element.50, f32[768]{0:T(1024)S(1)} %get-tuple-element.51, f32[1024]{0:T(1024)S(1)} %fusion.15, ...), kind=kOutput, calls=%fused_computation.12 | convolution fusion | flops 4838916096 | bytes 14173184 | tf_op jit(solution)/shard_map/td,tf->df/dot_general | solution.py:1296
  171.0 13.0 %fusion.9 = (f32[768]{0:T(1024)S(1)}, bf16[1024,768]{1,0:T(8,128)(2,1)}, f32[1024]{0:T(1024)S(1)}, f32[1024,768]{1,0:T(8,128)}, bf16[1024,768]{1,0:T(8,128)(2,1)S(1)}) fusion(bf16[4,256,768]{2,1,0:T(8,128)(2,1)S(1)} %copy-done.6, f32[1024,768]{1,0:T(8,128)S(1)} %get-tuple-element.58, f32[768]{0:T(1024)S(1)} %get-tuple-element.48, ...), kind=kOutput, calls=%fused_computation.21 | convolution fusion | flops 4872730624 | bytes 31485952 | tf_op jit(solution)/shard_map/tf,fd->td/dot_general | solution.py:1296
  184.0 10.3 %convolution_convert_fusion = bf16[3072,768]{1,0:T(8,128)(2,1)S(1)} fusion(bf16[1024,768]{1,0:T(8,128)(2,1)S(1)} %get-tuple-element.72, f32[1024,3072]{1,0:T(8,128)} %fusion.20), kind=kOutput, calls=%fused_computation.11 | convolution fusion | flops 4862509056 | bytes 18874368 | tf_op jit(solution)/shard_map/tf,td->fd/dot_general | solution.py:1296
  194.4 2.5 fusion.24
  196.9 1.1 copy-done.12
  197.9 0.6 multiply_reduce_fusion.2
  198.6 0.6 concatenate.43.refs_14_
  199.2 4.0 %convolution_convert_fusion.2.refs_5_ = bf16[1024,768]{1,0:T(8,128)(2,1)} fusion(bf16[768,768]{1,0:T(8,128)(2,1)} %bitcast.61, f32[1024,768]{1,0:T(8,128)S(1)} %get-tuple-element.54, f32[768]{0:T(1024)S(1)} %get-tuple-element.52), kind=kOutput, calls=%fused_computation.31 | convolution fusion | flops 1210318848 | bytes 5901312 | tf_op jit(solution)/shard_map/te,de->td/dot_general | solution.py:1296
  203.2 1.5 convolution_convert_fusion.3
  204.7 1.3 convert_element_type.84.refs_12_
  206.0 1.2 constant_dynamic-update-slice_fusion.7
  207.2 2.6 constant_dynamic-update-slice_fusion.6
  209.8 1.2 constant_dynamic-update-slice_fusion.5
  211.0 1.1 constant_dynamic-update-slice_fusion.4
  212.2 1.2 constant_dynamic-update-slice_fusion.3
  213.3 1.2 constant_dynamic-update-slice_fusion.2.refs_0_
  214.5 125.8 %shard_map.214 = (f32[24,2304]{1,0:T(8,128)}, f32[24,768]{1,0:T(8,128)}, f32[24,3072]{1,0:T(8,128)}, f32[96,768]{1,0:T(8,128)}, bf16[3,256,768]{2,1,0:T(8,128)(2...) custom-call(bf16[2,2,2,4,24,6912]{5,4,3,2,1,0:T(8,128)(2,1)} %constant_dynamic-update-slice_fusion.2.refs_0_, ...), custom_call_target="tpu_custom_call" | custom-call | tf_op jit(solution)/shard_map/pallas_call | solution.py:1253
  340.3 1.3 reduce_sum.107
  341.6 0.6 fusion.16
  342.2 0.6 dynamic_slice.17
  342.8 1.3 copy.26
  344.1 0.0 copy-start.1
  344.1 1.2 fusion.10
  345.4 1.0 copy.48
  346.4 1.0 copy.49
  347.4 0.7 copy.50
  348.1 0.6 copy.51
  348.7 0.7 copy.52
  349.5 0.7 copy.53
  (63 shorter events, 0.2 us)
Async XLA Ops:
  0.6 19.5 %copy-start = (bf16[24,4608]{1,0:T(8,128)(2,1)S(1)}, bf16[24,4608]{1,0:T(8,128)(2,1)}, u32[]{:S(2)}) copy-start(bf16[24,4608]{1,0:T(8,128)(2,1)} %param.17) | copy-start | bytes 663556
  20.1 1.4 copy-start.16
  117.5 6.5 %copy-start.2 = (bf16[8,4,24,6912]{3,2,1,0:T(8,128)(2,1)S(1)}, bf16[8,4,24,6912]{3,2,1,0:T(8,128)(2,1)}, u32[]{:S(2)}) copy-start(bf16[8,4,24,6912]{3,2,1,0:T(8,128)(2,1)} %get-tuple-element.30) | copy-start | bytes 31850500
  124.7 1.3 copy-start.7
  125.3 1.4 copy-start.3
  125.3 1.9 copy-start.4
  129.4 8.4 %copy-start.13 = (bf16[4,256,768]{2,1,0:T(8,128)(2,1)S(1)}, bf16[4,256,768]{2,1,0:T(8,128)(2,1)}, u32[]{:S(2)}) copy-start(bf16[4,256,768]{2,1,0:T(8,128)(2,1)} %fusion.7) | copy-start | bytes 4718596
  153.2 10.0 %copy-start.21 = (bf16[1024,3072]{1,0:T(8,128)(2,1)S(1)}, bf16[1024,3072]{1,0:T(8,128)(2,1)}, u32[]{:S(2)}) copy-start(bf16[1024,3072]{1,0:T(8,128)(2,1)} %fusion.6) | copy-start | bytes 18874372
  163.3 7.7 %copy-start.6 = (bf16[4,256,768]{2,1,0:T(8,128)(2,1)S(1)}, bf16[4,256,768]{2,1,0:T(8,128)(2,1)}, u32[]{:S(2)}) copy-start(bf16[4,256,768]{2,1,0:T(8,128)(2,1)} %get-tuple-element.28) | copy-start | bytes 4718596
  163.3 7.7 %copy-start.22 = (f32[1024,768]{1,0:T(8,128)S(1)}, f32[1024,768]{1,0:T(8,128)}, u32[]{:S(2)}) copy-start(f32[1024,768]{1,0:T(8,128)} %get-tuple-element.78) | copy-start | bytes 9437188
  194.3 3.6 %copy-start.12 = (f32[1024,768]{1,0:T(8,128)S(1)}, f32[1024,768]{1,0:T(8,128)}, u32[]{:S(2)}) copy-start(f32[1024,768]{1,0:T(8,128)} %get-tuple-element.71) | copy-start | bytes 9437188
  199.2 4.0 %copy-start.5 = (bf16[1024,768]{1,0:T(8,128)(2,1)S(1)}, bf16[1024,768]{1,0:T(8,128)(2,1)}, u32[]{:S(2)}) copy-start(bf16[1024,768]{1,0:T(8,128)(2,1)} %get-tuple-element.27.refs_4_) | copy-start | bytes 4718596
  199.2 8.0 %slice-start = ((s8[4718592]{0:T(1024)(128)(4,1)}), s8[4194304]{0:T(1024)(128)(4,1)S(1)}, s32[]{:S(2)}) async-start(s8[4718592]{0:T(1024)(128)(4,1)} %bitcast.66), calls=%async_computation | async-start | bytes 8388608
  203.2 4.0 %slice-start.1 = ((s8[4718592]{0:T(1024)(128)(4,1)}), s8[524288]{0:T(1024)(128)(4,1)S(1)}, s32[]{:S(2)}) async-start(s8[4718592]{0:T(1024)(128)(4,1)} %bitcast.66), calls=%async_computation.1 | async-start | bytes 1048576
  207.2 2.7 copy-start.11
  207.2 3.8 %copy-start.10 = (bf16[8,4,24,768]{3,2,1,0:T(8,128)(2,1)S(1)}, bf16[8,4,24,768]{3,2,1,0:T(8,128)(2,1)}, u32[]{:S(2)}) copy-start(bf16[8,4,24,768]{3,2,1,0:T(8,128)(2,1)} %get-tuple-element.66) | copy-start | bytes 3538948
  209.8 2.3 copy-start.9
  209.8 3.5 copy-start.8
  340.3 5.1 %copy-start.15 = (bf16[3,256,768]{2,1,0:T(8,128)(2,1)S(1)}, bf16[3,256,768]{2,1,0:T(8,128)(2,1)}, u32[]{:S(2)}) copy-start(bf16[3,256,768]{2,1,0:T(8,128)(2,1)} %get-tuple-element.91) | copy-start | bytes 3538948
  340.3 6.1 %copy-start.14 = (bf16[3,256,768]{2,1,0:T(8,128)(2,1)S(1)}, bf16[3,256,768]{2,1,0:T(8,128)(2,1)}, u32[]{:S(2)}) copy-start(bf16[3,256,768]{2,1,0:T(8,128)(2,1)} %get-tuple-element.92) | copy-start | bytes 3538948
  342.8 4.6 %copy-start.19 = (f32[24,2304]{1,0:T(8,128)S(1)}, f32[24,2304]{1,0:T(8,128)}, u32[]{:S(2)}) copy-start(f32[24,2304]{1,0:T(8,128)} %get-tuple-element.96) | copy-start | bytes 663556
  344.1 4.0 %copy-start.20 = (f32[24,768]{1,0:T(8,128)S(1)}, f32[24,768]{1,0:T(8,128)}, u32[]{:S(2)}) copy-start(f32[24,768]{1,0:T(8,128)} %get-tuple-element.97) | copy-start | bytes 221188
  344.1 4.6 %copy-start.18 = (f32[24,3072]{1,0:T(8,128)S(1)}, f32[24,3072]{1,0:T(8,128)}, u32[]{:S(2)}) copy-start(f32[24,3072]{1,0:T(8,128)} %get-tuple-element.99) | copy-start | bytes 884740
  344.1 6.0 %copy-start.1 = (bf16[24,4608]{1,0:T(8,128)(2,1)S(1)}, bf16[24,4608]{1,0:T(8,128)(2,1)}, u32[]{:S(2)}) copy-start(bf16[24,4608]{1,0:T(8,128)(2,1)} %param.17) | copy-start | bytes 663556
  345.4 4.1 %copy-start.17 = (f32[96,768]{1,0:T(8,128)S(1)}, f32[96,768]{1,0:T(8,128)}, u32[]{:S(2)}) copy-start(f32[96,768]{1,0:T(8,128)} %get-tuple-element.100) | copy-start | bytes 884740
